TPU v7x, 256 devices: a whole 4x4x8 slice. The times are simulated.
256 devices in a mesh: dp: 8 (over y, core), cent: 32 (over x, z).
Axes of the slice: x: 4, y: 4, z: 8, core: 2. Of those that a mesh axis runs over, the one named last changes fastest.
Arguments:
- batch: bfloat16 [2, 32768, 768], P(None, ('dp', 'cent')), may hold values from -16 to 16
- centroids: float32 [16384, 768], P('cent'), may hold values from -0.25 to 0.25
- counts: float32 [16384], P('cent'), may hold values from 4 to 32
Outputs:
- refined_centroids: float32 [16384, 768], P('cent')
- new_counts: float32 [16384], P('cent')
All inputs are finite; a program needn't handle non-finite values.
Results may differ from a plain program's by a relative error of at most 0.011.
Values may be sent and summed in bfloat16 or wider, within the bound.
A program may use at most 128 MiB of HBM per device.

v0:
```python
import jax
import jax.numpy as jnp
from jax import lax
from jax.sharding import PartitionSpec as P

sharpness_factor = 4.0


def body(batch, centroids, counts):
    current = centroids
    mass = counts
    for step in range(batch.shape[0]):
        input_rows = lax.all_gather(batch[step], "cent", axis=0, tiled=True)
        quantized_values = current.astype(jnp.bfloat16)
        affinity_scores = (
            jnp.dot(input_rows, quantized_values.T, preferred_element_type=jnp.float32)
            * sharpness_factor
        )
        local_peak = jnp.max(affinity_scores, axis=1)
        peak = lax.pmax(local_peak, "cent")
        powers = jnp.exp(affinity_scores - peak[:, None])
        total = lax.psum(jnp.sum(powers, axis=1), "cent")
        resp = (powers / total[:, None]).astype(jnp.bfloat16)
        sums = jnp.dot(resp.T, input_rows, preferred_element_type=jnp.float32)
        gained = jnp.sum(resp.astype(jnp.float32), axis=0)
        whole_sums, whole_gain = lax.psum((sums, gained), "dp")
        current = (mass[:, None] * current + whole_sums) / (mass + whole_gain)[:, None]
        mass = mass + whole_gain
    return (current, mass)


def solution(mesh):
    return jax.shard_map(
        body,
        mesh=mesh,
        in_specs=(P(None, ("dp", "cent"), None), P("cent", None), P("cent")),
        out_specs=(P("cent", None), P("cent")),
        check_vma=False,
    )
```

profile of v0, /device:TPU:1, one launch (start us, length us, event | category | flops | bytes accessed | tf_op | source)
XLA Modules:
  0.0 845.9 jit_solution(3966758147458474462)
XLA Ops:
  7.2 0.0 all-gather.5.cloned.1.call-start
  7.2 1.8 fusion.12
  9.0 0.0 all-gather.5.cloned.1.call-update
  9.0 0.0 all-gather.7.cloned.1.call-start
  9.1 0.7 all-gather.7.cloned.1.call-update
  9.8 0.0 all-reduce.3.cloned.1.call-start
  9.8 93.5 %all-gather.5.cloned.1.call-done = bf16[1,4096,768]{2,1,0:T(8,128)(2,1)} async-done(((bf16[1,128,768]{2,1,0:T(8,128)(2,1)}), bf16[1,4096,768]{2,1,0:T(8,128)(2,1)}) %all-gather.5.cloned.1.call-update) | async-done | bytes 6291472 | tf_op jit(solution)/shard_map/all_gather | solution.py:13
  103.3 9.9 %multiply_reduce_fusion.1 = (f32[4096]{0:T(1024)S(1)}, f32[4096,512]{0,1:T(8,128)}) fusion(f32[512,768]{1,0:T(8,128)} %param.4, bf16[1,4096,768]{2,1,0:T(8,128)(2,1)} %all-gather.5.cloned.1.call-done), kind=kOutput, calls=%fused_computation.7 | convolution fusion | flops 3225808896 | bytes 16269312 | tf_op jit(solution)/shard_map/dot_general | solution.py:16
  113.2 112.3 %pmax.14 = f32[4096]{0:T(1024)S(1)} all-reduce(f32[4096]{0:T(1024)S(1)} %get-tuple-element.8), channel_id=1, replica_groups=mesh['dp'=8,'cent'=32] {'cent'}, use_global_device_ids=true, to_apply=%region_1.0 | all-reduce | flops 4096 | bytes 32768 | tf_op jit(solution)/shard_map/pmax | solution.py:20
  225.5 4.8 fusion
  230.2 110.4 %psum.42 = f32[4096]{0:T(1024)S(1)} all-reduce(f32[4096]{0:T(1024)S(1)} %fusion), channel_id=1, replica_groups=mesh['dp'=8,'cent'=32] {'cent'}, use_global_device_ids=true, to_apply=%region_3.0 | all-reduce | flops 4096 | bytes 32768 | tf_op jit(solution)/shard_map/psum | solution.py:22
  340.6 4.7 convert_reduce_fusion.1
  345.3 0.0 copy-start.2
  345.3 0.0 copy-start
  345.3 6.7 fusion.6
  352.1 0.0 all-reduce.3.cloned.1.call-update
  352.1 0.0 all-reduce.5.cloned.1.call-start
  352.1 68.2 %psum.43 = f32[512]{0:T(512)S(1)} all-reduce(f32[512]{0:T(512)S(1)} %get-tuple-element.4), channel_id=1, replica_groups=mesh['dp'=8,'cent'=32] {'dp'}, use_global_device_ids=true, to_apply=%region_5.0 | all-reduce | flops 512 | bytes 4096 | tf_op jit(solution)/shard_map/psum | solution.py:26
  420.3 0.0 copy-done.2
  420.3 0.0 all-gather.7.cloned.1.call-done
  420.3 48.6 %all-reduce.3.cloned.1.call-done = f32[512,768]{1,0:T(8,128)} async-done(((f32[512,768]{1,0:T(8,128)}), f32[512,768]{1,0:T(8,128)}) %all-reduce.3.cloned.1.call-update) | async-done | bytes 1572880 | tf_op jit(solution)/shard_map/psum | solution.py:26
  468.9 0.0 copy-done
  468.9 10.0 %multiply_reduce_fusion = (f32[4096]{0:T(1024)S(1)}, f32[512,4096]{1,0:T(8,128)}) fusion(bf16[1,4096,768]{2,1,0:T(8,128)(2,1)} %all-gather.7.cloned.1.call-done, f32[512]{0:T(512)S(1)} %add.26, f32[512,768]{1,0:T(8,128)} %all-reduce.3.cloned.1.call-done, f32[512,768]{1,0:T(8,128)S(1)} %copy-done, f32[512]{0:T(512)S(1)} %copy-done.2), kind=kOutput, calls=%fused_computation.6 | convolution fusion | flops 3226988544 | bytes 17846272 | tf_op jit(solution)/shard_map/dot_general | solution.py:16
  478.9 115.5 %pmax.15 = f32[4096]{0:T(1024)S(1)} all-reduce(f32[4096]{0:T(1024)S(1)} %get-tuple-element.10), channel_id=1, replica_groups=mesh['dp'=8,'cent'=32] {'cent'}, use_global_device_ids=true, to_apply=%region_8.0 | all-reduce | flops 4096 | bytes 32768 | tf_op jit(solution)/shard_map/pmax | solution.py:20
  594.4 4.8 fusion.1
  599.1 110.9 %psum.45 = f32[4096]{0:T(1024)S(1)} all-reduce(f32[4096]{0:T(1024)S(1)} %fusion.1), channel_id=1, replica_groups=mesh['dp'=8,'cent'=32] {'cent'}, use_global_device_ids=true, to_apply=%region_10.0 | all-reduce | flops 4096 | bytes 32768 | tf_op jit(solution)/shard_map/psum | solution.py:22
  710.0 4.7 convert_reduce_fusion
  714.7 0.0 copy-start.1
  714.7 6.7 fusion.2
  721.4 0.0 all-reduce.5.cloned.1.call-update
  721.5 69.0 %psum.47 = f32[512]{0:T(512)S(1)} all-reduce(f32[512]{0:T(512)S(1)} %get-tuple-element.2), channel_id=1, replica_groups=mesh['dp'=8,'cent'=32] {'dp'}, use_global_device_ids=true, to_apply=%region_13.0 | all-reduce | flops 512 | bytes 4096 | tf_op jit(solution)/shard_map/psum | solution.py:26
  790.5 0.0 copy-start.3
  790.5 45.9 %all-reduce.5.cloned.1.call-done = f32[512,768]{1,0:T(8,128)} async-done(((f32[512,768]{1,0:T(8,128)}), f32[512,768]{1,0:T(8,128)}) %all-reduce.5.cloned.1.call-update) | async-done | bytes 1572880 | tf_op jit(solution)/shard_map/psum | solution.py:26
  836.4 0.0 copy-done.1
  836.4 3.0 add_divide_fusion
  839.4 0.0 copy-done.3
  (2 shorter events, 0.0 us)
Async XLA Ops:
  7.2 96.1 %all-gather.5.cloned.1.call-start = ((), (), s32[]{:S(2)}) async-start(), calls=%async_computation.2 | async-start | bytes 6488064 | tf_op jit(solution)/shard_map/all_gather | solution.py:13
  9.0 411.3 %all-gather.7.cloned.1.call-start = ((), (), s32[]{:S(2)}) async-start(), calls=%async_computation.3 | async-start | bytes 6488064 | tf_op jit(solution)/shard_map/all_gather | solution.py:13
  9.8 459.1 %all-reduce.3.cloned.1.call-start = ((), (), s32[]{:S(2)}) async-start(), calls=%async_computation | async-start | bytes 3145728 | tf_op jit(solution)/shard_map/psum | solution.py:26
  345.3 75.0 %copy-start.2 = (f32[512]{0:T(512)S(1)}, f32[512]{0:T(512)}, u32[]{:S(2)}) copy-start(f32[512]{0:T(512)} %param.5) | copy-start | bytes 6148
  345.3 123.6 %copy-start = (f32[512,768]{1,0:T(8,128)S(1)}, f32[512,768]{1,0:T(8,128)}, u32[]{:S(2)}) copy-start(f32[512,768]{1,0:T(8,128)} %param.4) | copy-start | bytes 4718596
  352.1 484.4 %all-reduce.5.cloned.1.call-start = ((), (), s32[]{:S(2)}) async-start(), calls=%async_computation.1 | async-start | bytes 3145728 | tf_op jit(solution)/shard_map/psum | solution.py:26
  714.7 121.8 %copy-start.1 = (f32[512,768]{1,0:T(8,128)S(1)}, f32[512,768]{1,0:T(8,128)}, u32[]{:S(2)}) copy-start(f32[512,768]{1,0:T(8,128)} %all-reduce.3.cloned.1.call-done) | copy-start | bytes 4718596
  790.5 48.9 %copy-start.3 = (f32[512]{0:T(512)}, f32[512]{0:T(512)S(1)}, u32[]{:S(2)}) copy-start(f32[512]{0:T(512)S(1)} %add.29) | copy-start | bytes 6148
Sparse Core Ops, SparseCore 0:
  11.2 92.0 all-gather.4
  105.9 85.8 all-gather.6
  352.2 116.6 all-reduce.2
  721.6 114.8 all-reduce.4
where the time goes:
time: 847 us; the launch traced here: 846 us
  blocking collectives  586 us (69%)
  waiting for transfers between devices  189 us (22%)
  matrix products  33.4 us (4%)
  other arithmetic  21.8 us (3%)
  between operations  13.8 us (2%)
    pmax x2, blocking collectives, body(): peak = lax.pmax(local_peak, 'cent')  228 us
    psum x2, blocking collectives, body(): total = lax.psum(jnp.sum(powers, axis=1), 'cent')  221 us
    psum x2, blocking collectives, body(): whole_sums, whole_gain = lax.psum((sums, gained), 'dp')  137 us
    psum x2, waiting for transfers between devices, body(): whole_sums, whole_gain = lax.psum((sums, gained), 'dp')  94.5 us
    all_gather x2, waiting for transfers between devices, body(): input_rows = lax.all_gather(batch[step], 'cent', axis=0, tiled=True)  93.5 us
    dot_general x2, matrix products, body(): jnp.dot(input_rows, quantized_values.T, preferred_element_type=jnp.float32)  19.9 us
  transfers between devices with their start and end apart: 4, of which 3 were waited for; matrix products, arithmetic and copies ran while one was open for 3% of the time, Pallas kernels for 0%

commit v1 on v0

v1 whole, which is shorter than its diff:
```python
import jax
import jax.numpy as jnp
from jax import lax
from jax.experimental import pallas as pl
from jax.experimental.pallas import tpu as pltpu
from jax.sharding import PartitionSpec as P

MESH = pl.DeviceIdType.MESH
F32 = jnp.float32
BF16 = jnp.bfloat16
SHARP = 4.0

NX, NY, NZ = 4, 4, 8
OWN = 128
ROWS = NZ * OWN
D = 768
HALF = D // 2
BLOCK = 512
PART = BLOCK // 2
QUART = PART // NY
SEMS = 176


def kernel(batch, cents, counts, out, new_counts, rows, cbuf, pbuf, mst, lst, stats, own_sums, csend, crecv, abuf, arecv,
           bbuf, brecv, a2, a2recv, b2, b2recv, gbuf, grecv, gsum, g1recv, g2, g2recv, cur, massbuf, send_sem, recv_sem):
    dp = lax.axis_index("dp")
    ce = lax.axis_index("cent")
    y, k = dp // 2, dp % 2
    x, z = ce // NZ, ce % NZ

    def at(px, py, pz, pk):
        return (py * 2 + pk, px * NZ + pz)

    other = at(x, y, z, 1 - k)

    def xpeer(d):
        return at((x + d) % NX, y, z, k)

    def ypeer(d):
        return at(x, (y + d) % NY, z, k)

    def zpeer(d):
        return at(x, y, (z + d) % NZ, k)

    used = [0]
    sent = []

    def take(n=1):
        used[0] += n
        return used[0] - n

    def copy(src, dst, peer, sem):
        return pltpu.make_async_remote_copy(
            src_ref=src, dst_ref=dst, send_sem=send_sem.at[sem], recv_sem=recv_sem.at[sem],
            device_id=peer, device_id_type=MESH)

    def send(src, dst, peer):
        c = copy(src, dst, peer, take())
        c.start()
        sent.append(c)
        return c

    barrier = pltpu.get_barrier_semaphore()
    peers = [other]
    peers += [xpeer(d) for d in range(1, NX)]
    peers += [ypeer(d) for d in range(1, NY)]
    peers += [zpeer(d) for d in range(1, NZ)]
    for p in peers:
        pl.semaphore_signal(barrier, inc=1, device_id=p, device_id_type=MESH)

    mine = pl.ds(pl.multiple_of(z * OWN, OWN), OWN)
    for t in range(2):
        rows[t, mine, :] = batch[t]
    for h in range(2):
        cbuf[0, x, h] = (cents[h * PART:(h + 1) * PART, :] * SHARP).astype(BF16)

    pl.semaphore_wait(barrier, len(peers))

    def ring(t):
        arrived = {}

        def hop(h):
            for sign in (1, -1):
                for c in ((0, 1) if h < 4 else ((0,) if sign == 1 else (1,))):
                    if h > 1:
                        arrived.pop((h - 1, sign, c)).wait_recv()
                    owner = (z + NZ - sign * (h - 1)) % NZ
                    where = pl.ds(pl.multiple_of(owner * OWN + c * (OWN // 2), OWN // 2), OWN // 2)
                    arrived[(h, sign, c)] = send(rows.at[t, where], rows.at[t, where], zpeer(sign % NZ))

        def finish():
            for key in sorted(arrived):
                arrived.pop(key).wait_recv()

        return hop, finish

    hop, finish = ring(0)
    hop2, finish2 = ring(1)
    hop(1)
    first = [send(cbuf.at[0, x, k], cbuf.at[0, x, k], xpeer(d)) for d in range(1, NX)]
    hop(2)
    hop(3)
    hop(4)
    hop2(1)
    passed = []
    for i, d in enumerate(range(1, NX)):
        first[i].wait_recv()
        src = cbuf.at[0, (x + NX - d) % NX, k]
        passed.append(send(src, src, other))
    finish()
    for c in passed:
        c.wait_recv()

    def scores(t):
        def body(c, _):
            for h in range(2):
                s = lax.dot_general(cbuf[t, c, h], rows[t], (((1,), (1,)), ((), ())), preferred_element_type=F32)
                m = jnp.max(s, axis=0, keepdims=True)
                p = jnp.exp(s - m)
                mst[pl.ds(c * 2 + h, 1), :] = m
                lst[pl.ds(c * 2 + h, 1), :] = jnp.sum(p, axis=0, keepdims=True)
                pbuf[c, h] = p.astype(BF16)
            return 0

        lax.fori_loop(0, NX, body, 0)

    def normalise(t):
        m = mst[...]
        top = jnp.max(m, axis=0, keepdims=True)
        stats[t, z, 0:1, :] = top
        stats[t, z, 1:2, :] = jnp.sum(lst[...] * jnp.exp(m - top), axis=0, keepdims=True)
        around = [send(stats.at[t, z], stats.at[t, z], zpeer(d)) for d in range(1, NZ)]
        for c in around:
            c.wait_recv()
        peak = stats[t, 0, 0:1, :]
        for i in range(1, NZ):
            peak = jnp.maximum(peak, stats[t, i, 0:1, :])
        total = jnp.zeros_like(peak)
        for i in range(NZ):
            total = total + stats[t, i, 1:2, :] * jnp.exp(stats[t, i, 0:1, :] - peak)
        mst[...] = jnp.exp(m - peak) / total

    def reduce_sums(t, midway):
        to_core = take(NX)
        to_x = take(NX - 1)

        def core_copy(c, i):
            return copy(csend.at[t, c], crecv.at[t, c], other, to_core + i)

        def x_copy(c, i):
            return copy(abuf.at[t, c], arecv.at[t, i], at(c, y, z, k), to_x + i)

        def combine(i):
            c = (x + 1 + i) % NX
            core_copy(c, i).wait_recv()
            whole = own_sums[c] + crecv[t, c].astype(F32)
            abuf[t, c] = whole[:, :HALF].astype(BF16)
            bbuf[t, :, c] = whole[:, HALF:].astype(BF16).reshape(NY, QUART, HALF)

            @pl.when(i < NX - 1)
            def _():
                x_copy(c, i).start()

        def body(i, _):
            c = (x + 1 + i) % NX
            for h in range(2):
                resp = (pbuf[c, h].astype(F32) * mst[pl.ds(c * 2 + h, 1), :]).astype(BF16)
                pbuf[c, h] = resp
                wide = resp.astype(F32)
                acc = wide[:, :128]
                for j in range(1, ROWS // 128):
                    acc = acc + wide[:, j * 128:(j + 1) * 128]
                gbuf[t, c, h] = lax.dot_general(
                    jnp.ones((8, 128), F32), acc, (((1,), (1,)), ((), ())),
                    precision=lax.Precision.HIGHEST, preferred_element_type=F32)
            csend[t, c] = jnp.dot(pbuf[c, 1 - k], rows[t], preferred_element_type=F32).astype(BF16)
            core_copy(c, i).start()
            own_sums[c] = jnp.dot(pbuf[c, k], rows[t], preferred_element_type=F32)

            @pl.when(i > 0)
            def _():
                combine(i - 1)

            return 0

        lax.fori_loop(0, NX, body, 0)
        g_core = send(gbuf.at[t, :, 1 - k], grecv.at[t], other)
        combine(NX - 1)
        from_y = [
            send(bbuf.at[t, (y + d) % NY], brecv.at[t, d - 1], ypeer(d)) for d in range(1, NY)]
        g_core.wait_recv()
        for c in range(NX):
            gsum[t, c] = gbuf[t, c, k] + grecv[t, c]
        g_x = [send(gsum.at[t, (x + d) % NX], g1recv.at[t, d - 1], xpeer(d)) for d in range(1, NX)]
        midway()

        for i in range(NX - 1):
            x_copy((x + 1 + i) % NX, i).wait_recv()
        part_a = abuf[t, x].astype(F32)
        for i in range(NX - 1):
            part_a = part_a + arecv[t, i].astype(F32)
        a2[t] = part_a.reshape(NY, QUART, HALF)
        sends_a = []
        for d in range(1, NY):
            a2recv[t, 3 + d - 1] = a2[t, (y + d) % NY].astype(BF16)
            sends_a.append(send(a2recv.at[t, 3 + d - 1], a2recv.at[t, d - 1], ypeer(d)))
        for c in from_y:
            c.wait_recv()
        part_b = bbuf[t, y].astype(F32)
        for i in range(NY - 1):
            part_b = part_b + brecv[t, i].astype(F32)
        b2[t] = part_b
        sends_b = []
        for d in range(1, NX):
            b2recv[t, 3 + d - 1] = b2[t, (x + d) % NX].astype(BF16)
            sends_b.append(send(b2recv.at[t, 3 + d - 1], b2recv.at[t, d - 1], xpeer(d)))
        for c in g_x:
            c.wait_recv()
        g = gsum[t, x]
        for i in range(NX - 1):
            g = g + g1recv[t, i]
        g2[t] = g
        g_y = [send(g2.at[t], g2recv.at[t, d - 1], ypeer(d)) for d in range(1, NY)]
        for c in sends_a:
            c.wait_recv()
        sum_a = a2[t, y]
        for i in range(NY - 1):
            sum_a = sum_a + a2recv[t, i].astype(F32)
        for c in sends_b:
            c.wait_recv()
        sum_b = b2[t, x]
        for i in range(NX - 1):
            sum_b = sum_b + b2recv[t, i].astype(F32)
        for c in g_y:
            c.wait_recv()
        for i in range(NY - 1):
            g = g + g2recv[t, i]
        for i in range(NX):
            core_copy((x + 1 + i) % NX, i).wait_send()
        for i in range(NX - 1):
            x_copy((x + 1 + i) % NX, i).wait_send()
        return sum_a, sum_b, g

    quarter = pl.ds(pl.multiple_of(y * QUART, QUART), QUART)
    place = pl.ds(pl.multiple_of(k * PART + y * QUART, QUART), QUART)
    lane = lax.broadcasted_iota(jnp.int32, (QUART, PART), 1)
    line = lax.broadcasted_iota(jnp.int32, (QUART, PART), 0) + y * QUART
    hit = lane == line

    def column(v):
        return jnp.sum(jnp.where(hit, v[0:1, :], 0.0), axis=1, keepdims=True)

    def update(old, mass, sum_a, sum_b, g):
        m = column(mass)
        down = m + column(g)
        return (m * old[:, :HALF] + sum_a) / down, (m * old[:, HALF:] + sum_b) / down

    scores(0)
    hop2(2)
    normalise(0)
    sum_a, sum_b, g = reduce_sums(0, lambda: hop2(3))
    mass = jnp.broadcast_to(counts[pl.ds(k, 1), :], (8, PART))
    left, right = update(cents[place, :], mass, sum_a, sum_b, g)
    mass = mass + g
    massbuf[0, k] = mass
    cur[:, :HALF] = left
    cur[:, HALF:] = right
    cbuf[1, x, k, quarter, :HALF] = (left * SHARP).astype(BF16)
    cbuf[1, x, k, quarter, HALF:] = (right * SHARP).astype(BF16)

    lo, hi = pl.ds(0, HALF), pl.ds(HALF, HALF)
    own_left = cbuf.at[1, x, k, quarter, lo]
    own_right = cbuf.at[1, x, k, quarter, hi]
    left1 = [send(own_left, own_left, ypeer(d)) for d in range(1, NY)]
    right1 = [send(own_right, own_right, xpeer(d)) for d in range(1, NX)]
    hop2(4)
    for c in left1:
        c.wait_recv()
    all_left = cbuf.at[1, x, k, :, lo]
    left2 = [send(all_left, all_left, xpeer(d)) for d in range(1, NX)]
    for c in right1:
        c.wait_recv()
    all_right = cbuf.at[1, :, k, quarter, hi]
    right2 = [send(all_right, all_right, ypeer(d)) for d in range(1, NY)]
    passed = [send(all_left, all_left, other), send(all_right, all_right, other)]
    finish2()
    for i, d in enumerate(range(1, NX)):
        left2[i].wait_recv()
        src = cbuf.at[1, (x + NX - d) % NX, k, :, lo]
        passed.append(send(src, src, other))
        right2[i].wait_recv()
        src = cbuf.at[1, :, k, pl.ds(pl.multiple_of(((y + NY - d) % NY) * QUART, QUART), QUART), hi]
        passed.append(send(src, src, other))
    for c in passed:
        c.wait_recv()

    scores(1)
    normalise(1)
    sum_a, sum_b, g = reduce_sums(1, lambda: None)
    mass = massbuf[0, k]
    left, right = update(cur[...], mass, sum_a, sum_b, g)
    out[place, :HALF] = left
    out[place, HALF:] = right
    around = [send(out.at[place], out.at[place], ypeer(d)) for d in range(1, NY)]
    passed = [send(out.at[place], out.at[place], other)]
    massbuf[1, k] = mass + g
    passed.append(send(massbuf.at[1, k], massbuf.at[1, k], other))
    for i, d in enumerate(range(1, NY)):
        around[i].wait_recv()
        src = out.at[pl.ds(pl.multiple_of(k * PART + ((y + NY - d) % NY) * QUART, QUART), QUART)]
        passed.append(send(src, src, other))
    for c in passed:
        c.wait_recv()
    new_counts[0:1, :] = massbuf[1, 0, 0:1, :]
    new_counts[1:2, :] = massbuf[1, 1, 0:1, :]
    for c in sent:
        c.wait_send()
    assert used[0] <= SEMS, used[0]


def body(batch, centroids, counts):
    vmem = pl.BlockSpec(memory_space=pltpu.VMEM)
    refined, mass = pl.pallas_call(
        kernel,
        out_shape=(
            jax.ShapeDtypeStruct((BLOCK, D), F32),
            jax.ShapeDtypeStruct((2, PART), F32),
        ),
        in_specs=[vmem] * 3,
        out_specs=(vmem, vmem),
        scratch_shapes=[
            pltpu.VMEM((2, ROWS, D), BF16),
            pltpu.VMEM((2, NX, 2, PART, D), BF16),
            pltpu.VMEM((NX, 2, PART, ROWS), BF16),
            pltpu.VMEM((2 * NX, ROWS), F32),
            pltpu.VMEM((2 * NX, ROWS), F32),
            pltpu.VMEM((2, NZ, 2, ROWS), F32),
            pltpu.VMEM((NX, PART, D), F32),
            pltpu.VMEM((2, NX, PART, D), BF16),
            pltpu.VMEM((2, NX, PART, D), BF16),
            pltpu.VMEM((2, NX, PART, HALF), BF16),
            pltpu.VMEM((2, NX - 1, PART, HALF), BF16),
            pltpu.VMEM((2, NY, NX, QUART, HALF), BF16),
            pltpu.VMEM((2, NY - 1, NX, QUART, HALF), BF16),
            pltpu.VMEM((2, NY, QUART, HALF), F32),
            pltpu.VMEM((2, 6, QUART, HALF), BF16),
            pltpu.VMEM((2, NX, QUART, HALF), F32),
            pltpu.VMEM((2, 6, QUART, HALF), BF16),
            pltpu.VMEM((2, NX, 2, 8, PART), F32),
            pltpu.VMEM((2, NX, 8, PART), F32),
            pltpu.VMEM((2, NX, 8, PART), F32),
            pltpu.VMEM((2, NX - 1, 8, PART), F32),
            pltpu.VMEM((2, 8, PART), F32),
            pltpu.VMEM((2, NY - 1, 8, PART), F32),
            pltpu.VMEM((QUART, D), F32),
            pltpu.VMEM((2, 2, 8, PART), F32),
            pltpu.SemaphoreType.DMA((SEMS,)),
            pltpu.SemaphoreType.DMA((SEMS,)),
        ],
        compiler_params=pltpu.CompilerParams(
            collective_id=0, has_side_effects=True, vmem_limit_bytes=58 * 1024 * 1024
        ),
    )(batch, centroids, counts.reshape(2, PART))
    return refined, mass.reshape(BLOCK)


def solution(mesh):
    return jax.shard_map(
        body,
        mesh=mesh,
        in_specs=(P(None, ("dp", "cent"), None), P("cent", None), P("cent")),
        out_specs=(P("cent", None), P("cent")),
        check_vma=False,
    )
```

time: 847 us -> 145 us (0.17)
  blocking collectives: 586 us -> 0 us
  waiting for transfers between devices: 189 us -> 0 us
  Pallas kernels: 0 us -> 139 us
  matrix products: 33.4 us -> 0 us
  other arithmetic: 21.8 us -> 0 us
  between operations: 13.8 us -> 0.64 us
    psum x4 -> x0, blocking collectives: 358 us -> none  [the longest x2 221 us: body(): total = lax.psum(jnp.sum(powers, axis=1), 'cent')]
    pmax x2 -> x0, blocking collectives: 228 us -> none  [body(): peak = lax.pmax(local_peak, 'cent')]
    pallas_call x0 -> x1, Pallas kernels: none -> 139 us  [body(): pl.pallas_call(kernel, out_shape=(jax.ShapeDtypeStruct((BLOCK, D), F32),...]
    psum x2 -> x0, waiting for transfers between devices: 94.5 us -> none  [body(): whole_sums, whole_gain = lax.psum((sums, gained), 'dp')]
    all_gather x2 -> x0, waiting for transfers between devices: 93.5 us -> none  [body(): input_rows = lax.all_gather(batch[step], 'cent', axis=0, tiled=True)]
    dot_general x4 -> x0, matrix products: 33.4 us -> none  [the longest x2 19.9 us: body(): jnp.dot(input_rows, quantized_values.T, preferred_element_type=jnp.float32)]
    reduce_sum x4 -> x0, other arithmetic: 18.9 us -> none  [the longest x2 9.53 us: body(): total = lax.psum(jnp.sum(powers, axis=1), 'cent')]
  transfers between devices with their start and end apart: 4 -> 0, of which waited for: 3 -> 0; matrix products, arithmetic and copies ran while one was open for 3% -> 0% of each run, Pallas kernels for 0% -> 0%
where the time goes in v1:
time: 145 us
  Pallas kernels  139 us (96%)
  local copies, waits for them, and re-layouts  5.17 us (4%)
    pallas_call x1, Pallas kernels, body(): pl.pallas_call(kernel, out_shape=(jax.ShapeDtypeStruct((BLOCK, D), F32),...  139 us
    unnamed x2, local copies, waits for them, and re-layouts  3.9 us

profile of v1, /device:TPU:1, one launch (start us, length us, event | category | flops | bytes accessed | tf_op | source)
XLA Modules:
  0.0 144.9 jit_solution(9879674307789961632)
XLA Ops:
  0.6 1.3 reshape.10.counts
  1.9 139.1 %shard_map.50 = (f32[512,768]{1,0:T(8,128)}, f32[2,256]{1,0:T(2,128)}) custom-call(bf16[2,128,768]{2,1,0:T(8,128)(2,1)} %batch.1, f32[512,768]{1,0:T(8,128)} %cents.1, f32[2,256]{1,0:T(2,128)} %reshape.10.counts), custom_call_target="tpu_custom_call" | custom-call | tf_op jit(solution)/shard_map/pallas_call | solution.py:323
  141.0 1.3 copy.5
  142.3 2.7 %copy.7 = f32[512,768]{1,0:T(8,128)} copy(f32[512,768]{1,0:T(8,128)} %get-tuple-element.8) | data formatting | bytes 3145728

commit v2 on v0

v2 whole, which is shorter than its diff:
```python
import jax
import jax.numpy as jnp
from jax import lax
from jax.experimental import pallas as pl
from jax.experimental.pallas import tpu as pltpu
from jax.sharding import PartitionSpec as P

MESH = pl.DeviceIdType.MESH
F32 = jnp.float32
BF16 = jnp.bfloat16
SHARP = 4.0

NX, NY, NZ = 4, 4, 8
OWN = 128
ROWS = NZ * OWN
D = 768
BLOCK = 512
PART = BLOCK // 2
QUART = PART // NY
ITEM = QUART // 2
SHARE = 4 * ITEM
SEMS = 160


def kernel(batch, cents, counts, out, new_counts, rows, cbuf, pbuf, mst, lst, stats, sums, crecv, abuf, arecv,
           a2, a2f, a2recv, gbuf, glin, grecv, gsum, g1recv, g2, g2recv, cur, massbuf, send_sem, recv_sem):
    dp = lax.axis_index("dp")
    ce = lax.axis_index("cent")
    y, k = dp // 2, dp % 2
    x, z = ce // NZ, ce % NZ
    me = (x, y)

    def at(px, py, pz, pk):
        return (py * 2 + pk, px * NZ + pz)

    other = at(x, y, z, 1 - k)

    def xpeer(d):
        return at((x + d) % NX, y, z, k)

    def ypeer(d):
        return at(x, (y + d) % NY, z, k)

    def zpeer(d):
        return at(x, y, (z + d) % NZ, k)

    peer = (xpeer, ypeer)
    used = [0]
    sent = []

    def take(n=1):
        used[0] += n
        return used[0] - n

    def copy(src, dst, to, sem):
        return pltpu.make_async_remote_copy(
            src_ref=src, dst_ref=dst, send_sem=send_sem.at[sem], recv_sem=recv_sem.at[sem],
            device_id=to, device_id_type=MESH)

    def send(src, dst, to):
        c = copy(src, dst, to, take())
        c.start()
        sent.append(c)
        return c

    def items(i):
        return pl.ds(pl.multiple_of(i * ITEM, ITEM), ITEM)

    barrier = pltpu.get_barrier_semaphore()
    peers = [other]
    peers += [xpeer(d) for d in range(1, NX)]
    peers += [ypeer(d) for d in range(1, NY)]
    peers += [zpeer(d) for d in range(1, NZ)]
    for p in peers:
        pl.semaphore_signal(barrier, inc=1, device_id=p, device_id_type=MESH)

    mine = pl.ds(pl.multiple_of(z * OWN, OWN), OWN)
    for t in range(2):
        rows[t, mine, :] = batch[t]

    def from_block(first):
        return (cents[pl.ds(pl.multiple_of(k * PART + first, ITEM), ITEM), :] * SHARP).astype(BF16)

    for q in range(NY):
        cbuf[0, 0, x, k, q * ITEM:(q + 1) * ITEM, :] = from_block(q * QUART)
    cbuf[0, 1, y, k, items(x), :] = from_block(y * QUART + ITEM)

    pl.semaphore_wait(barrier, len(peers))

    def ring(t):
        arrived = {}

        def hop(h):
            for sign in (1, -1):
                for c in ((0, 1) if h < 4 else ((0,) if sign == 1 else (1,))):
                    if h > 1:
                        arrived.pop((h - 1, sign, c)).wait_recv()
                    owner = (z + NZ - sign * (h - 1)) % NZ
                    where = pl.ds(pl.multiple_of(owner * OWN + c * (OWN // 2), OWN // 2), OWN // 2)
                    arrived[(h, sign, c)] = send(rows.at[t, where], rows.at[t, where], zpeer(sign % NZ))

        def finish():
            for key in sorted(arrived):
                arrived.pop(key).wait_recv()

        return hop, finish

    def spread(t):
        near = take(6)
        far = take(6)
        over = take(8)

        def small(ty, d):
            src = cbuf.at[t, ty, me[ty], k, items(me[1 - ty])]
            return copy(src, src, peer[1 - ty](d), near + ty * 3 + d - 1)

        def large(ty, d):
            src = cbuf.at[t, ty, me[ty], k]
            return copy(src, src, peer[ty](d), far + ty * 3 + d - 1)

        def on(ty, d):
            src = cbuf.at[t, ty, (me[ty] + 4 - d) % 4, k]
            return copy(src, src, other, over + ty * 4 + d)

        def first(ty):
            for d in (2, 1, 3):
                small(ty, d).start()

        def second(ty, wait=True):
            if wait:
                for d in (1, 3, 2):
                    small(ty, d).wait()
            for d in (2, 1, 3):
                large(ty, d).start()

        def arrive(d, own):
            for ty in range(2):
                if not own:
                    large(ty, d).wait_recv()
                on(ty, d).start()

        def finish():
            for ty in range(2):
                for d in range(1, 4):
                    large(ty, d).wait_send()
                for d in range(4):
                    on(ty, d).wait_send()

        return first, second, arrive, on, finish

    def score(t, ty, i):
        s = lax.dot_general(
            cbuf[t, ty, i].reshape(2 * SHARE, D), rows[t], (((1,), (1,)), ((), ())), preferred_element_type=F32)
        m = jnp.max(s, axis=0, keepdims=True)
        p = jnp.exp(s - m)
        mst[pl.ds(ty * 4 + i, 1), :] = m
        lst[pl.ds(ty * 4 + i, 1), :] = jnp.sum(p, axis=0, keepdims=True)
        pbuf[ty, i] = p.astype(BF16).reshape(2, SHARE, ROWS)

    def near_first(j):
        return j + j // 2 - 2 * (j // 3)

    def normalise(t):
        m = mst[...]
        top = jnp.max(m, axis=0, keepdims=True)
        stats[t, z, 0:1, :] = top
        stats[t, z, 1:2, :] = jnp.sum(lst[...] * jnp.exp(m - top), axis=0, keepdims=True)
        around = [send(stats.at[t, z], stats.at[t, z], zpeer(d)) for d in (4, 3, 5, 2, 6, 1, 7)]
        for c in around:
            c.wait_recv()
        peak = stats[t, 0, 0:1, :]
        for i in range(1, NZ):
            peak = jnp.maximum(peak, stats[t, i, 0:1, :])
        total = jnp.zeros_like(peak)
        for i in range(NZ):
            total = total + stats[t, i, 1:2, :] * jnp.exp(stats[t, i, 0:1, :] - peak)
        mst[...] = jnp.exp(m - peak) / total

    def reduce_sums(t, midway):
        to_core = take(8)
        to_plane = take(6)

        def core_copy(ty, i, j):
            return copy(sums.at[ty, i, 1 - k], crecv.at[t, ty, i], other, to_core + ty * 4 + j)

        def plane_copy(ty, i, d):
            return copy(abuf.at[t, ty, i], arecv.at[t, ty, d - 1], peer[ty](d), to_plane + ty * 3 + d - 1)

        def far_first(j):
            return (2 + j * (j + 1) // 2) % 4

        def combine(j):
            d = far_first(j)
            for ty in range(2):
                i = (me[ty] + d) % 4
                core_copy(ty, i, j).wait_recv()
                whole = sums[ty, i, k] + crecv[t, ty, i]
                sums[ty, i, k] = whole
                abuf[t, ty, i] = whole.astype(BF16)

                @pl.when(j < 3)
                def _():
                    plane_copy(ty, i, d).start()

        def body(j, _):
            d = far_first(j)
            for ty in range(2):
                i = (me[ty] + d) % 4
                f = mst[pl.ds(ty * 4 + i, 1), :]
                for h in range(2):
                    resp = (pbuf[ty, i, h].astype(F32) * f).astype(BF16)
                    pbuf[ty, i, h] = resp
                    wide = resp.astype(F32)
                    acc = wide[:, :128]
                    for n in range(1, ROWS // 128):
                        acc = acc + wide[:, n * 128:(n + 1) * 128]
                    gbuf[ty, i, h] = jnp.broadcast_to(jnp.sum(acc.T, axis=0, keepdims=True), (8, SHARE))
                both = jnp.dot(pbuf[ty, i].reshape(2 * SHARE, ROWS), rows[t], preferred_element_type=F32)
                sums[ty, i] = both.reshape(2, SHARE, D)
                core_copy(ty, i, j).start()

            @pl.when(j > 0)
            def _():
                combine(j - 1)

            return 0

        lax.fori_loop(0, 4, body, 0)
        for h in range(2):
            for b in range(NX):
                for q in range(NY):
                    glin[t, h, b, :, q * QUART:q * QUART + ITEM] = gbuf[0, b, h, :, q * ITEM:(q + 1) * ITEM]
                    glin[t, h, b, :, q * QUART + ITEM:(q + 1) * QUART] = gbuf[1, q, h, :, b * ITEM:(b + 1) * ITEM]
        g_core = send(glin.at[t, 1 - k], grecv.at[t], other)
        combine(3)
        midway(0)
        g_core.wait_recv()
        for c in range(NX):
            gsum[t, c] = glin[t, k, c] + grecv[t, c]
        g_x = [send(gsum.at[t, (x + d) % NX], g1recv.at[t, d - 1], xpeer(d)) for d in range(1, NX)]

        second = []
        for ty in range(2):
            for d in range(1, 4):
                plane_copy(ty, (me[ty] + d) % 4, d).wait()
            part = sums[ty, me[ty], k]
            for n in range(3):
                part = part + arecv[t, ty, n].astype(F32)
            a2f[ty] = part.reshape(4, ITEM, D)
            a2[t, ty] = part.astype(BF16).reshape(4, ITEM, D)
            second.append([
                send(a2.at[t, ty, (me[1 - ty] + d) % 4], a2recv.at[t, ty, d - 1], peer[1 - ty](d)) for d in (2, 1, 3)])
        midway(1)
        for c in g_x:
            c.wait_recv()
        g = gsum[t, x]
        for n in range(NX - 1):
            g = g + g1recv[t, n]
        g2[t] = g
        g_y = [send(g2.at[t], g2recv.at[t, d - 1], ypeer(d)) for d in range(1, NY)]
        quarter = []
        for ty in range(2):
            for c in second[ty]:
                c.wait_recv()
            whole = a2f[ty, me[1 - ty]]
            for n in range(3):
                whole = whole + a2recv[t, ty, n].astype(F32)
            quarter.append(whole)
        for c in g_y:
            c.wait_recv()
        for n in range(NY - 1):
            g = g + g2recv[t, n]
        for j in range(4):
            for ty in range(2):
                core_copy(ty, (me[ty] + far_first(j)) % 4, j).wait_send()
        return jnp.concatenate(quarter, axis=0), g

    place = pl.ds(pl.multiple_of(k * PART + y * QUART, QUART), QUART)
    lane = lax.broadcasted_iota(jnp.int32, (QUART, PART), 1)
    line = lax.broadcasted_iota(jnp.int32, (QUART, PART), 0) + y * QUART
    hit = lane == line

    def column(v):
        return jnp.sum(jnp.where(hit, v[0:1, :], 0.0), axis=1, keepdims=True)

    def update(old, mass, total, g):
        m = column(mass)
        return (m * old + total) / (m + column(g))

    hop, finish = ring(0)
    hop2, finish2 = ring(1)
    first, second, arrive, on, finish_spread = spread(0)
    hop(1)
    first(1)
    second(0, wait=False)
    hop(2)
    second(1)
    hop(3)
    arrive(0, True)
    hop(4)
    for d in (1, 3, 2):
        arrive(d, False)
    finish()

    def early(j, _):
        d = near_first(j)
        for ty in range(2):
            on(ty, d).wait_recv()
            score(0, ty, (me[ty] + 4 - d) % 4)
        return 0

    lax.fori_loop(0, 4, early, 0)
    finish_spread()
    normalise(0)
    hop2(1)
    total, g = reduce_sums(0, lambda n: hop2(2 + n))
    mass = jnp.broadcast_to(counts[pl.ds(k, 1), :], (8, PART))
    fresh = update(cents[place, :], mass, total, g)
    cur[...] = fresh
    massbuf[0, k] = mass + g
    fresh = (fresh * SHARP).astype(BF16)
    cbuf[1, 0, x, k, items(y), :] = fresh[:ITEM]
    cbuf[1, 1, y, k, items(x), :] = fresh[ITEM:]
    first, second, arrive, on, finish_spread = spread(1)
    first(0)
    first(1)
    hop2(4)
    second(0)
    second(1)
    finish2()

    def late(j, _):
        d = near_first(j)

        @pl.when(j == 0)
        def _():
            arrive(d, True)

        @pl.when((j > 0) & (j < 4))
        def _():
            arrive(d, False)

        @pl.when(j > 0)
        def _():
            before = near_first(j - 1)
            for ty in range(2):
                on(ty, before).wait_recv()
                score(1, ty, (me[ty] + 4 - before) % 4)

        return 0

    lax.fori_loop(0, 5, late, 0)
    finish_spread()
    normalise(1)
    total, g = reduce_sums(1, lambda n: None)
    mass = massbuf[0, k]
    out[place, :] = update(cur[...], mass, total, g).astype(BF16)
    around = [send(out.at[place], out.at[place], ypeer(d)) for d in (2, 1, 3)]
    passed = [send(out.at[place], out.at[place], other)]
    massbuf[1, k] = mass + g
    passed.append(send(massbuf.at[1, k], massbuf.at[1, k], other))
    for n, d in ((1, 1), (2, 3), (0, 2)):
        around[n].wait_recv()
        src = out.at[pl.ds(pl.multiple_of(k * PART + ((y + NY - d) % NY) * QUART, QUART), QUART)]
        passed.append(send(src, src, other))
    for c in passed:
        c.wait_recv()
    new_counts[0:1, :] = massbuf[1, 0, 0:1, :]
    new_counts[1:2, :] = massbuf[1, 1, 0:1, :]
    for c in sent:
        c.wait_send()
    assert used[0] <= SEMS, used[0]


def body(batch, centroids, counts):
    vmem = pl.BlockSpec(memory_space=pltpu.VMEM)
    refined, mass = pl.pallas_call(
        kernel,
        out_shape=(
            jax.ShapeDtypeStruct((BLOCK, D), BF16),
            jax.ShapeDtypeStruct((2, PART), F32),
        ),
        in_specs=[vmem] * 3,
        out_specs=(vmem, vmem),
        scratch_shapes=[
            pltpu.VMEM((2, ROWS, D), BF16),
            pltpu.VMEM((2, 2, 4, 2, SHARE, D), BF16),
            pltpu.VMEM((2, 4, 2, SHARE, ROWS), BF16),
            pltpu.VMEM((8, ROWS), F32),
            pltpu.VMEM((8, ROWS), F32),
            pltpu.VMEM((2, NZ, 2, ROWS), F32),
            pltpu.VMEM((2, 4, 2, SHARE, D), F32),
            pltpu.VMEM((2, 2, 4, SHARE, D), F32),
            pltpu.VMEM((2, 2, 4, SHARE, D), BF16),
            pltpu.VMEM((2, 2, 3, SHARE, D), BF16),
            pltpu.VMEM((2, 2, 4, ITEM, D), BF16),
            pltpu.VMEM((2, 4, ITEM, D), F32),
            pltpu.VMEM((2, 2, 3, ITEM, D), BF16),
            pltpu.VMEM((2, 4, 2, 8, SHARE), F32),
            pltpu.VMEM((2, 2, NX, 8, PART), F32),
            pltpu.VMEM((2, NX, 8, PART), F32),
            pltpu.VMEM((2, NX, 8, PART), F32),
            pltpu.VMEM((2, NX - 1, 8, PART), F32),
            pltpu.VMEM((2, 8, PART), F32),
            pltpu.VMEM((2, NY - 1, 8, PART), F32),
            pltpu.VMEM((QUART, D), F32),
            pltpu.VMEM((2, 2, 8, PART), F32),
            pltpu.SemaphoreType.DMA((SEMS,)),
            pltpu.SemaphoreType.DMA((SEMS,)),
        ],
        compiler_params=pltpu.CompilerParams(
            collective_id=0, has_side_effects=True, vmem_limit_bytes=58 * 1024 * 1024
        ),
    )(batch, centroids, counts.reshape(2, PART))
    return refined.astype(F32), mass.reshape(BLOCK)


def solution(mesh):
    return jax.shard_map(
        body,
        mesh=mesh,
        in_specs=(P(None, ("dp", "cent"), None), P("cent", None), P("cent")),
        out_specs=(P("cent", None), P("cent")),
        check_vma=False,
    )
```

time: 847 us -> 126 us (0.15)
  blocking collectives: 586 us -> 0 us
  waiting for transfers between devices: 189 us -> 0 us
  Pallas kernels: 0 us -> 120 us
  matrix products: 33.4 us -> 0 us
  other arithmetic: 21.8 us -> 2.38 us
  between operations: 13.8 us -> 0.64 us
    psum x4 -> x0, blocking collectives: 358 us -> none  [the longest x2 221 us: body(): total = lax.psum(jnp.sum(powers, axis=1), 'cent')]
    pmax x2 -> x0, blocking collectives: 228 us -> none  [body(): peak = lax.pmax(local_peak, 'cent')]
    pallas_call x0 -> x1, Pallas kernels: none -> 120 us  [body(): pl.pallas_call(kernel, out_shape=(jax.ShapeDtypeStruct((BLOCK, D), BF16),...]
    psum x2 -> x0, waiting for transfers between devices: 94.5 us -> none  [body(): whole_sums, whole_gain = lax.psum((sums, gained), 'dp')]
    all_gather x2 -> x0, waiting for transfers between devices: 93.5 us -> none  [body(): input_rows = lax.all_gather(batch[step], 'cent', axis=0, tiled=True)]
    dot_general x4 -> x0, matrix products: 33.4 us -> none  [the longest x2 19.9 us: body(): jnp.dot(input_rows, quantized_values.T, preferred_element_type=jnp.float32)]
    reduce_sum x4 -> x0, other arithmetic: 18.9 us -> none  [the longest x2 9.53 us: body(): total = lax.psum(jnp.sum(powers, axis=1), 'cent')]
  transfers between devices with their start and end apart: 4 -> 0, of which waited for: 3 -> 0; matrix products, arithmetic and copies ran while one was open for 3% -> 0% of each run, Pallas kernels for 0% -> 0%
where the time goes in v2:
time: 126 us
  Pallas kernels  120 us (95%)
  local copies, waits for them, and re-layouts  2.53 us (2%)
  other arithmetic  2.38 us (2%)
    pallas_call x1, Pallas kernels, body(): pl.pallas_call(kernel, out_shape=(jax.ShapeDtypeStruct((BLOCK, D), BF16),...  120 us

profile of v2, /device:TPU:1, one launch (start us, length us, event | category | flops | bytes accessed | tf_op | source)
XLA Modules:
  0.0 125.5 jit_solution(5967319495207105513)
XLA Ops:
  0.6 1.3 %reshape.10.counts = f32[2,256]{1,0:T(2,128)} reshape(f32[512]{0:T(512)} %param.5) | data formatting | bytes 4096 | tf_op jit(solution)/shard_map/reshape | solution.py:414
  1.9 120.0 %shard_map.50 = (bf16[512,768]{1,0:T(8,128)(2,1)}, f32[2,256]{1,0:T(2,128)}) custom-call(bf16[2,128,768]{2,1,0:T(8,128)(2,1)} %batch.1, f32[512,768]{1,0:T(8,128)} %cents.1, f32[2,256]{1,0:T(2,128)} %reshape.10.counts), custom_call_target="tpu_custom_call" | custom-call | tf_op jit(solution)/shard_map/pallas_call | solution.py:377
  121.9 1.3 copy.5
  123.2 2.4 %convert_element_type.3 = f32[512,768]{1,0:T(8,128)} convert(bf16[512,768]{1,0:T(8,128)(2,1)} %get-tuple-element.4) | non-fusion elementwise | flops 393216 | bytes 2359296 | tf_op jit(solution)/shard_map/convert_element_type | solution.py:415

commit v3 on v2

v3 whole, which is shorter than its diff:
```python
import jax
import jax.numpy as jnp
from jax import lax
from jax.experimental import pallas as pl
from jax.experimental.pallas import tpu as pltpu
from jax.sharding import PartitionSpec as P

MESH = pl.DeviceIdType.MESH
F32 = jnp.float32
BF16 = jnp.bfloat16
SHARP = 4.0

NX, NY, NZ = 4, 4, 8
OWN = 128
ROWS = NZ * OWN
D = 768
BLOCK = 512
PART = BLOCK // 2
QUART = PART // NY
ITEM = QUART // 2
SHARE = 4 * ITEM
SEMS = 192
OWNERS = (-1, 1, -2, 2, -3, 3, 0, 4)


def kernel(batch, cents, counts, out, new_counts, rows, cbuf, pbuf, mst, lst, stats, joint, sums, crecv, abuf, arecv,
           a2, a2f, a2recv, gbuf, glin, grecv, gsum, g1recv, g2, g2recv, cur, massbuf, send_sem, recv_sem):
    dp = lax.axis_index("dp")
    ce = lax.axis_index("cent")
    y, k = dp // 2, dp % 2
    x, z = ce // NZ, ce % NZ
    me = (x, y)

    def at(px, py, pz, pk):
        return (py * 2 + pk, px * NZ + pz)

    other = at(x, y, z, 1 - k)

    def xpeer(d):
        return at((x + d) % NX, y, z, k)

    def ypeer(d):
        return at(x, (y + d) % NY, z, k)

    def zpeer(d):
        return at(x, y, (z + d) % NZ, k)

    peer = (xpeer, ypeer)
    used = [0]
    sent = []

    def take(n=1):
        used[0] += n
        return used[0] - n

    def copy(src, dst, to, sem):
        return pltpu.make_async_remote_copy(
            src_ref=src, dst_ref=dst, send_sem=send_sem.at[sem], recv_sem=recv_sem.at[sem],
            device_id=to, device_id_type=MESH)

    def send(src, dst, to):
        c = copy(src, dst, to, take())
        c.start()
        sent.append(c)
        return c

    def items(i):
        return pl.ds(pl.multiple_of(i * ITEM, ITEM), ITEM)

    barrier = pltpu.get_barrier_semaphore()
    peers = [other]
    peers += [xpeer(d) for d in range(1, NX)]
    peers += [ypeer(d) for d in range(1, NY)]
    peers += [zpeer(d) for d in range(1, NZ)]
    for p in peers:
        pl.semaphore_signal(barrier, inc=1, device_id=p, device_id_type=MESH)

    def slot(h, sign):
        return {0: 6, 4: 7}.get(h, 2 * h - 2 + (sign < 0)) * OWN

    for t in range(2):
        rows[t, slot(0, 1):slot(0, 1) + OWN, :] = batch[t]

    def from_block(first):
        return (cents[pl.ds(pl.multiple_of(k * PART + first, ITEM), ITEM), :] * SHARP).astype(BF16)

    for q in range(NY):
        cbuf[0, 0, x, k, q * ITEM:(q + 1) * ITEM, :] = from_block(q * QUART)
    cbuf[0, 1, y, k, items(x), :] = from_block(y * QUART + ITEM)

    pl.semaphore_wait(barrier, len(peers))

    def ring(t):
        arrived = {}

        def hop(h):
            for c in (0, 1):
                for sign in (1, -1):
                    if h == 4 and c != (sign < 0):
                        continue
                    if h > 1:
                        arrived.pop((h - 1, sign, c)).wait_recv()
                    src = pl.ds(slot(h - 1, sign) + c * (OWN // 2), OWN // 2)
                    dst = pl.ds(slot(h, sign) + c * (OWN // 2), OWN // 2)
                    arrived[(h, sign, c)] = send(rows.at[t, src], rows.at[t, dst], zpeer(sign % NZ))

        def finish(last=4):
            for key in sorted(arrived):
                if key[0] <= last:
                    arrived.pop(key).wait_recv()

        return hop, finish

    def spread(t):
        near_sem = take(6)
        far_sem = take(24)
        over = take(8)

        def near(ty, n):
            src = cbuf.at[t, ty, me[ty], k, items(me[1 - ty])]
            return copy(src, src, peer[1 - ty](n), near_sem + ty * 3 + n - 1)

        def far(ty, n, d, start=True):
            block = me[ty] if start else (me[ty] + 4 - d) % 4
            src = cbuf.at[t, ty, block, k, items((me[1 - ty] + 4 - n) % 4)]
            return copy(src, src, peer[ty](d), far_sem + ty * 12 + (d - 1) * 4 + n)

        def on(ty, d):
            src = cbuf.at[t, ty, (me[ty] + 4 - d) % 4, k]
            return copy(src, src, other, over + ty * 4 + d)

        def begin(types):
            for ty in types:
                for n in (2, 1, 3):
                    near(ty, n).start()
            for ty in range(2):
                for d in (2, 1, 3):
                    far(ty, 0, d).start()

        def go_on(types):
            for n in (1, 3, 2):
                for ty in types:
                    near(ty, n).wait()
            for d in (1, 3, 2):
                for n in (1, 3, 2):
                    for ty in range(2):
                        far(ty, n, d).start()

        def arrive(d, own):
            for ty in range(2):
                if not own:
                    for n in range(4):
                        far(ty, n, d, False).wait_recv()
                on(ty, d).start()

        def finish():
            for ty in range(2):
                for d in range(1, 4):
                    for n in range(4):
                        far(ty, n, d).wait_send()
                for d in range(4):
                    on(ty, d).wait_send()

        return begin, go_on, arrive, on, finish

    def score(t, ty, i, first, size):
        s = lax.dot_general(
            cbuf[t, ty, i].reshape(2 * SHARE, D), rows[t, first:first + size, :], (((1,), (1,)), ((), ())),
            preferred_element_type=F32)
        m = jnp.max(s, axis=0, keepdims=True)
        p = jnp.exp(s - m)
        mst[pl.ds(ty * 4 + i, 1), first:first + size] = m
        lst[pl.ds(ty * 4 + i, 1), first:first + size] = jnp.sum(p, axis=0, keepdims=True)
        pbuf[ty, i, :, :, first:first + size] = p.astype(BF16).reshape(2, SHARE, size)

    def near_first(j):
        return j + j // 2 - 2 * (j // 3)

    def normalise(t):
        m = mst[...]
        top = jnp.max(m, axis=0, keepdims=True)
        low = jnp.sum(lst[...] * jnp.exp(m - top), axis=0, keepdims=True)
        places = [pl.ds(pl.multiple_of((z + NZ + off) % NZ * OWN, OWN), OWN) for off in OWNERS]
        for b, where in enumerate(places):
            stats[t, z, 0:1, where] = top[:, b * OWN:(b + 1) * OWN]
            stats[t, z, 1:2, where] = low[:, b * OWN:(b + 1) * OWN]
        around = [send(stats.at[t, z], stats.at[t, z], zpeer(d)) for d in (4, 3, 5, 2, 6, 1, 7)]
        for c in around:
            c.wait_recv()
        peak = stats[t, 0, 0:1, :]
        for i in range(1, NZ):
            peak = jnp.maximum(peak, stats[t, i, 0:1, :])
        total = jnp.zeros_like(peak)
        for i in range(NZ):
            total = total + stats[t, i, 1:2, :] * jnp.exp(stats[t, i, 0:1, :] - peak)
        joint[0:1, :] = peak
        joint[1:2, :] = total
        for b, where in enumerate(places):
            joint[2:4, b * OWN:(b + 1) * OWN] = joint[0:2, where]
        mst[...] = jnp.exp(m - joint[2:3, :]) / joint[3:4, :]

    def reduce_sums(t, midway):
        to_core = take(8)
        to_plane = take(6)

        def core_copy(ty, j):
            i = target(ty, j)
            return copy(sums.at[ty, i, 1 - k], crecv.at[t, ty, i], other, to_core + ty * 4 + j)

        def plane_copy(ty, d):
            i = (x + ty * (y - x) + d) % 4
            to = at(x + (1 - ty) * (i - x), y + ty * (i - y), z, k)
            return copy(abuf.at[t, ty, i], arecv.at[t, ty, d - 1], to, to_plane + ty * 3 + d - 1)

        def far_first(j):
            return (2 + j * (j + 1) // 2) % 4

        def target(ty, j):
            return (x + ty * (y - x) + far_first(j)) % 4

        def combine(n):
            ty, j = n % 2, n // 2
            i = target(ty, j)
            core_copy(ty, j).wait_recv()
            whole = sums[ty, i, k] + crecv[t, ty, i]
            sums[ty, i, k] = whole
            abuf[t, ty, i] = whole.astype(BF16)

            @pl.when(j < 3)
            def _():
                plane_copy(ty, far_first(j)).start()

        def body(n, _):
            ty, j = n % 2, n // 2
            i = target(ty, j)
            f = mst[pl.ds(ty * 4 + i, 1), :]
            for h in range(2):
                pbuf[ty, i, h] = (pbuf[ty, i, h].astype(F32) * f).astype(BF16)
            both = jnp.dot(pbuf[ty, i].reshape(2 * SHARE, ROWS), rows[t], preferred_element_type=F32)
            sums[ty, i] = both.reshape(2, SHARE, D)
            core_copy(ty, j).start()

            @pl.when(n > 1)
            def _():
                combine(n - 2)

            return 0

        lax.fori_loop(0, 8, body, 0)
        combine(6)
        combine(7)

        def masses(n, _):
            ty, i = n // 4, n % 4
            for h in range(2):
                wide = pbuf[ty, i, h].astype(F32)
                acc = wide[:, :128]
                for b in range(1, ROWS // 128):
                    acc = acc + wide[:, b * 128:(b + 1) * 128]
                gbuf[ty, i, h] = jnp.broadcast_to(jnp.sum(acc.T, axis=0, keepdims=True), (8, SHARE))
            return 0

        lax.fori_loop(0, 8, masses, 0)
        for h in range(2):
            for b in range(NX):
                for q in range(NY):
                    glin[t, h, b, :, q * QUART:q * QUART + ITEM] = gbuf[0, b, h, :, q * ITEM:(q + 1) * ITEM]
                    glin[t, h, b, :, q * QUART + ITEM:(q + 1) * QUART] = gbuf[1, q, h, :, b * ITEM:(b + 1) * ITEM]
        g_core = send(glin.at[t, 1 - k], grecv.at[t], other)
        midway()
        g_core.wait_recv()
        for c in range(NX):
            gsum[t, c] = glin[t, k, c] + grecv[t, c]
        g_x = [send(gsum.at[t, (x + d) % NX], g1recv.at[t, d - 1], xpeer(d)) for d in range(1, NX)]

        second = []
        for ty in range(2):
            for d in range(1, 4):
                plane_copy(ty, d).wait()
            part = sums[ty, me[ty], k]
            for n in range(3):
                part = part + arecv[t, ty, n].astype(F32)
            a2f[ty] = part.reshape(4, ITEM, D)
            a2[t, ty] = part.astype(BF16).reshape(4, ITEM, D)
            second.append([
                send(a2.at[t, ty, (me[1 - ty] + d) % 4], a2recv.at[t, ty, d - 1], peer[1 - ty](d)) for d in (2, 1, 3)])
        for c in g_x:
            c.wait_recv()
        g = gsum[t, x]
        for n in range(NX - 1):
            g = g + g1recv[t, n]
        g2[t] = g
        g_y = [send(g2.at[t], g2recv.at[t, d - 1], ypeer(d)) for d in range(1, NY)]
        quarter = []
        for ty in range(2):
            for c in second[ty]:
                c.wait_recv()
            whole = a2f[ty, me[1 - ty]]
            for n in range(3):
                whole = whole + a2recv[t, ty, n].astype(F32)
            quarter.append(whole)
        for c in g_y:
            c.wait_recv()
        for n in range(NY - 1):
            g = g + g2recv[t, n]
        for j in range(4):
            for ty in range(2):
                core_copy(ty, j).wait_send()
        return jnp.concatenate(quarter, axis=0), g

    place = pl.ds(pl.multiple_of(k * PART + y * QUART, QUART), QUART)
    lane = lax.broadcasted_iota(jnp.int32, (QUART, PART), 1)
    line = lax.broadcasted_iota(jnp.int32, (QUART, PART), 0) + y * QUART
    hit = lane == line

    def column(v):
        return jnp.sum(jnp.where(hit, v[0:1, :], 0.0), axis=1, keepdims=True)

    def update(old, mass, total, g):
        m = column(mass)
        return (m * old + total) / (m + column(g))

    hop, finish = ring(0)
    hop2, finish2 = ring(1)
    begin, go_on, arrive, on, finish_spread = spread(0)
    hop(1)
    begin((1,))
    go_on((1,))
    arrive(0, True)
    hop(2)
    arrive(1, False)
    arrive(3, False)
    hop(3)
    arrive(2, False)
    hop(4)

    def early(b):
        first, size = b * 2 * OWN, 2 * OWN

        def some(ty, _):
            s = lax.dot_general(
                cbuf[0, ty].reshape(8 * SHARE, D), rows[0, first:first + size, :], (((1,), (1,)), ((), ())),
                preferred_element_type=F32)
            for i in range(4):
                part = s[i * 2 * SHARE:(i + 1) * 2 * SHARE]
                m = jnp.max(part, axis=0, keepdims=True)
                p = jnp.exp(part - m)
                mst[pl.ds(ty * 4 + i, 1), first:first + size] = m
                lst[pl.ds(ty * 4 + i, 1), first:first + size] = jnp.sum(p, axis=0, keepdims=True)
                pbuf[ty, i, :, :, first:first + size] = p.astype(BF16).reshape(2, SHARE, size)
            return 0

        lax.fori_loop(0, 2, some, 0)

    for d in (0, 1, 3, 2):
        for ty in range(2):
            on(ty, d).wait_recv()
    early(0)
    early(1)
    finish(3)
    early(2)
    finish()
    early(3)
    finish_spread()
    normalise(0)
    hop2(1)
    total, g = reduce_sums(0, lambda: hop2(2))
    mass = jnp.broadcast_to(counts[pl.ds(pl.multiple_of(k * PART, PART), PART)].reshape(1, PART), (8, PART))
    fresh = update(cents[place, :], mass, total, g)
    cur[...] = fresh
    massbuf[0, k] = mass + g
    fresh = (fresh * SHARP).astype(BF16)
    cbuf[1, 0, x, k, items(y), :] = fresh[:ITEM]
    cbuf[1, 1, y, k, items(x), :] = fresh[ITEM:]
    begin, go_on, arrive, on, finish_spread = spread(1)
    begin((0, 1))
    hop2(3)
    go_on((0, 1))
    hop2(4)
    finish2()

    def late(j, _):
        d = near_first(j)

        @pl.when(j == 0)
        def _():
            arrive(d, True)

        @pl.when((j > 0) & (j < 4))
        def _():
            arrive(d, False)

        @pl.when(j > 0)
        def _():
            before = near_first(j - 1)
            for ty in range(2):
                on(ty, before).wait_recv()
                score(1, ty, (me[ty] + 4 - before) % 4, 0, ROWS)

        return 0

    lax.fori_loop(0, 5, late, 0)
    finish_spread()
    normalise(1)
    total, g = reduce_sums(1, lambda: None)
    mass = massbuf[0, k]
    out[place, :] = update(cur[...], mass, total, g).astype(BF16)
    around = [send(out.at[place], out.at[place], ypeer(d)) for d in (2, 1, 3)]
    passed = [send(out.at[place], out.at[place], other)]
    massbuf[1, k] = mass + g
    passed.append(send(massbuf.at[1, k], massbuf.at[1, k], other))
    for n, d in ((1, 1), (2, 3), (0, 2)):
        around[n].wait_recv()
        src = out.at[pl.ds(pl.multiple_of(k * PART + ((y + NY - d) % NY) * QUART, QUART), QUART)]
        passed.append(send(src, src, other))
    for c in passed:
        c.wait_recv()
    for h in range(2):
        new_counts[h * PART:(h + 1) * PART] = massbuf[1, h][0]
    for c in sent:
        c.wait_send()
    assert used[0] <= SEMS, used[0]


def body(batch, centroids, counts):
    vmem = pl.BlockSpec(memory_space=pltpu.VMEM)
    refined, mass = pl.pallas_call(
        kernel,
        out_shape=(
            jax.ShapeDtypeStruct((BLOCK, D), BF16),
            jax.ShapeDtypeStruct((BLOCK,), F32),
        ),
        in_specs=[vmem] * 3,
        out_specs=(vmem, vmem),
        scratch_shapes=[
            pltpu.VMEM((2, ROWS, D), BF16),
            pltpu.VMEM((2, 2, 4, 2, SHARE, D), BF16),
            pltpu.VMEM((2, 4, 2, SHARE, ROWS), BF16),
            pltpu.VMEM((8, ROWS), F32),
            pltpu.VMEM((8, ROWS), F32),
            pltpu.VMEM((2, NZ, 2, ROWS), F32),
            pltpu.VMEM((4, ROWS), F32),
            pltpu.VMEM((2, 4, 2, SHARE, D), F32),
            pltpu.VMEM((2, 2, 4, SHARE, D), F32),
            pltpu.VMEM((2, 2, 4, SHARE, D), BF16),
            pltpu.VMEM((2, 2, 3, SHARE, D), BF16),
            pltpu.VMEM((2, 2, 4, ITEM, D), BF16),
            pltpu.VMEM((2, 4, ITEM, D), F32),
            pltpu.VMEM((2, 2, 3, ITEM, D), BF16),
            pltpu.VMEM((2, 4, 2, 8, SHARE), F32),
            pltpu.VMEM((2, 2, NX, 8, PART), F32),
            pltpu.VMEM((2, NX, 8, PART), F32),
            pltpu.VMEM((2, NX, 8, PART), F32),
            pltpu.VMEM((2, NX - 1, 8, PART), F32),
            pltpu.VMEM((2, 8, PART), F32),
            pltpu.VMEM((2, NY - 1, 8, PART), F32),
            pltpu.VMEM((QUART, D), F32),
            pltpu.VMEM((2, 2, 8, PART), F32),
            pltpu.SemaphoreType.DMA((SEMS,)),
            pltpu.SemaphoreType.DMA((SEMS,)),
        ],
        compiler_params=pltpu.CompilerParams(
            collective_id=0, has_side_effects=True, vmem_limit_bytes=44 * 1024 * 1024
        ),
    )(batch, centroids, counts)
    return refined.astype(F32), mass


def solution(mesh):
    return jax.shard_map(
        body,
        mesh=mesh,
        in_specs=(P(None, ("dp", "cent"), None), P("cent", None), P("cent")),
        out_specs=(P("cent", None), P("cent")),
        check_vma=False,
    )
```

time: 126 us -> 116 us (0.921)
  Pallas kernels: 120 us -> 110 us
    pallas_call x1, Pallas kernels: 120 us -> 110 us  [body(): pl.pallas_call(kernel, out_shape=(jax.ShapeDtypeStruct((BLOCK, D), BF16),...]
    unnamed x1 -> x7, local copies, waits for them, and re-layouts: 1.25 us -> 3.66 us
    reshape x1 -> x0, local copies, waits for them, and re-layouts: 1.27 us -> none  [body(): counts.reshape(2, PART)]
where the time goes in v3:
time: 116 us
  Pallas kernels  110 us (95%)
  local copies, waits for them, and re-layouts  3.66 us (3%)
  other arithmetic  1.25 us (1%)
    pallas_call x1, Pallas kernels, body(): pl.pallas_call(kernel, out_shape=(jax.ShapeDtypeStruct((BLOCK, D), BF16),...  110 us
    unnamed x7, local copies, waits for them, and re-layouts  3.66 us

profile of v3, /device:TPU:1, one launch (start us, length us, event | category | flops | bytes accessed | tf_op | source)
XLA Modules:
  0.0 116.0 jit_solution(11533270664916866382)
XLA Ops:
  0.6 0.0 copy-start
  0.6 1.4 %copy-done = f32[512,768]{1,0:T(8,128)S(1)} copy-done((f32[512,768]{1,0:T(8,128)S(1)}, f32[512,768]{1,0:T(8,128)}, u32[]{:S(2)}) %copy-start) | copy-done | bytes 1572888
  2.0 0.0 copy-start.1
  2.0 1.0 copy-done.1
  3.0 0.0 copy-start.2
  3.0 0.7 copy-done.2
  3.7 110.4 %shard_map.50 = (bf16[512,768]{1,0:T(8,128)(2,1)S(1)}, f32[512]{0:T(512)S(1)}) custom-call(bf16[2,128,768]{2,1,0:T(8,128)(2,1)S(1)} %copy-done.1, f32[512,768]{1,0:T(8,128)S(1)} %copy-done, f32[512]{0:T(512)S(1)} %copy-done.2), custom_call_target="tpu_custom_call" | custom-call | tf_op jit(solution)/shard_map/pallas_call | solution.py:427
  114.1 1.3 %convert_element_type.3 = f32[512,768]{1,0:T(8,128)} convert(bf16[512,768]{1,0:T(8,128)(2,1)S(1)} %get-tuple-element.4) | non-fusion elementwise | flops 393216 | bytes 2359296 | tf_op jit(solution)/shard_map/convert_element_type | solution.py:466
  115.4 0.6 copy.6
Async XLA Ops:
  0.6 1.4 %copy-start = (f32[512,768]{1,0:T(8,128)S(1)}, f32[512,768]{1,0:T(8,128)}, u32[]{:S(2)}) copy-start(f32[512,768]{1,0:T(8,128)} %cents.1) | copy-start | bytes 4718596
  2.0 1.0 copy-start.1
  3.0 0.7 copy-start.2

commit v4 on v3

--- a/solution.py
+++ b/solution.py
@@ -19,7 +19,7 @@
 QUART = PART // NY
 ITEM = QUART // 2
 SHARE = 4 * ITEM
-SEMS = 192
+SENDS, RECVS = 20, 80
 OWNERS = (-1, 1, -2, 2, -3, 3, 0, 4)
 
 
@@ -46,23 +46,29 @@
         return at(x, y, (z + d) % NZ, k)
 
     peer = (xpeer, ypeer)
-    used = [0]
-    sent = []
-
-    def take(n=1):
-        used[0] += n
-        return used[0] - n
-
-    def copy(src, dst, to, sem):
+    used = [0, 0]
+
+    def take(n):
+        used[1] += n
+        return used[1] - n
+
+    def sender():
+        used[0] += 1
+        return used[0] - 1
+
+    def copy(src, dst, to, group, sem):
         return pltpu.make_async_remote_copy(
-            src_ref=src, dst_ref=dst, send_sem=send_sem.at[sem], recv_sem=recv_sem.at[sem],
+            src_ref=src, dst_ref=dst, send_sem=send_sem.at[group], recv_sem=recv_sem.at[sem],
             device_id=to, device_id_type=MESH)
 
-    def send(src, dst, to):
-        c = copy(src, dst, to, take())
-        c.start()
-        sent.append(c)
-        return c
+    def wait_sent(size, group):
+        copy(size, size, other, group, 0).wait_send()
+
+    def wait_arrived(size, sem):
+        copy(size, size, other, 0, sem).wait_recv()
+
+    def lines(n):
+        return rows.at[0, pl.ds(0, n)]
 
     def items(i):
         return pl.ds(pl.multiple_of(i * ITEM, ITEM), ITEM)
@@ -90,44 +96,51 @@
 
     pl.semaphore_wait(barrier, len(peers))
 
-    def ring(t):
+    ring_from, ring_sem = sender(), take(28)
+
+    def ring(t, parts):
+        size = OWN // parts
         arrived = {}
+        count = [0]
 
         def hop(h):
-            for c in (0, 1):
+            for c in range(parts):
                 for sign in (1, -1):
-                    if h == 4 and c != (sign < 0):
+                    if h == 4 and (c >= parts // 2) != (sign < 0):
                         continue
                     if h > 1:
-                        arrived.pop((h - 1, sign, c)).wait_recv()
-                    src = pl.ds(slot(h - 1, sign) + c * (OWN // 2), OWN // 2)
-                    dst = pl.ds(slot(h, sign) + c * (OWN // 2), OWN // 2)
-                    arrived[(h, sign, c)] = send(rows.at[t, src], rows.at[t, dst], zpeer(sign % NZ))
+                        arrived.pop((h - 1, c, sign)).wait_recv()
+                    src = pl.ds(slot(h - 1, sign) + c * size, size)
+                    dst = pl.ds(slot(h, sign) + c * size, size)
+                    going = copy(rows.at[t, src], rows.at[t, dst], zpeer(sign % NZ), ring_from, ring_sem + count[0])
+                    going.start()
+                    count[0] += 1
+                    arrived[(h, c, sign)] = going
 
         def finish(last=4):
             for key in sorted(arrived):
                 if key[0] <= last:
                     arrived.pop(key).wait_recv()
+            if last == 4:
+                wait_sent(lines(7 * OWN), ring_from)
 
         return hop, finish
 
+    near_from, far_from, over_from = sender(), sender(), sender()
+    near_sem, far_sem, over_sem = take(2), take(6), take(8)
+
     def spread(t):
-        near_sem = take(6)
-        far_sem = take(24)
-        over = take(8)
-
         def near(ty, n):
             src = cbuf.at[t, ty, me[ty], k, items(me[1 - ty])]
-            return copy(src, src, peer[1 - ty](n), near_sem + ty * 3 + n - 1)
-
-        def far(ty, n, d, start=True):
-            block = me[ty] if start else (me[ty] + 4 - d) % 4
-            src = cbuf.at[t, ty, block, k, items((me[1 - ty] + 4 - n) % 4)]
-            return copy(src, src, peer[ty](d), far_sem + ty * 12 + (d - 1) * 4 + n)
+            return copy(src, src, peer[1 - ty](n), near_from, near_sem + ty)
+
+        def far(ty, n, d):
+            src = cbuf.at[t, ty, me[ty], k, items((me[1 - ty] + 4 - n) % 4)]
+            return copy(src, src, peer[ty](d), far_from, far_sem + ty * 3 + d - 1)
 
         def on(ty, d):
             src = cbuf.at[t, ty, (me[ty] + 4 - d) % 4, k]
-            return copy(src, src, other, over + ty * 4 + d)
+            return copy(src, src, other, over_from, over_sem + ty * 4 + d)
 
         def begin(types):
             for ty in types:
@@ -138,9 +151,8 @@
                     far(ty, 0, d).start()
 
         def go_on(types):
-            for n in (1, 3, 2):
-                for ty in types:
-                    near(ty, n).wait()
+            for ty in types:
+                wait_arrived(lines(3 * ITEM), near_sem + ty)
             for d in (1, 3, 2):
                 for n in (1, 3, 2):
                     for ty in range(2):
@@ -149,17 +161,13 @@
         def arrive(d, own):
             for ty in range(2):
                 if not own:
-                    for n in range(4):
-                        far(ty, n, d, False).wait_recv()
+                    wait_arrived(lines(SHARE), far_sem + ty * 3 + d - 1)
                 on(ty, d).start()
 
-        def finish():
-            for ty in range(2):
-                for d in range(1, 4):
-                    for n in range(4):
-                        far(ty, n, d).wait_send()
-                for d in range(4):
-                    on(ty, d).wait_send()
+        def finish(types):
+            wait_sent(lines(3 * ITEM * len(types)), near_from)
+            wait_sent(lines(6 * SHARE), far_from)
+            wait_sent(lines(8 * SHARE), over_from)
 
         return begin, go_on, arrive, on, finish
 
@@ -184,9 +192,11 @@
         for b, where in enumerate(places):
             stats[t, z, 0:1, where] = top[:, b * OWN:(b + 1) * OWN]
             stats[t, z, 1:2, where] = low[:, b * OWN:(b + 1) * OWN]
-        around = [send(stats.at[t, z], stats.at[t, z], zpeer(d)) for d in (4, 3, 5, 2, 6, 1, 7)]
-        for c in around:
-            c.wait_recv()
+        group, sem = sender(), take(1)
+        for d in (4, 3, 5, 2, 6, 1, 7):
+            copy(stats.at[t, z], stats.at[t, z], zpeer(d), group, sem).start()
+        wait_arrived(stats.at[t, pl.ds(0, NZ - 1)], sem)
+        wait_sent(stats.at[t, pl.ds(0, NZ - 1)], group)
         peak = stats[t, 0, 0:1, :]
         for i in range(1, NZ):
             peak = jnp.maximum(peak, stats[t, i, 0:1, :])
@@ -199,18 +209,19 @@
             joint[2:4, b * OWN:(b + 1) * OWN] = joint[0:2, where]
         mst[...] = jnp.exp(m - joint[2:3, :]) / joint[3:4, :]
 
+    core_from, plane_from, second_from, mass_from = sender(), sender(), sender(), sender()
+    core_sem, plane_sem, second_sem, mass_sem = take(8), take(2), take(2), take(3)
+
     def reduce_sums(t, midway):
-        to_core = take(8)
-        to_plane = take(6)
 
         def core_copy(ty, j):
             i = target(ty, j)
-            return copy(sums.at[ty, i, 1 - k], crecv.at[t, ty, i], other, to_core + ty * 4 + j)
+            return copy(sums.at[ty, i, 1 - k], crecv.at[t, ty, i], other, core_from, core_sem + ty * 4 + j)
 
         def plane_copy(ty, d):
             i = (x + ty * (y - x) + d) % 4
             to = at(x + (1 - ty) * (i - x), y + ty * (i - y), z, k)
-            return copy(abuf.at[t, ty, i], arecv.at[t, ty, d - 1], to, to_plane + ty * 3 + d - 1)
+            return copy(abuf.at[t, ty, i], arecv.at[t, ty, d - 1], to, plane_from, plane_sem + ty)
 
         def far_first(j):
             return (2 + j * (j + 1) // 2) % 4
@@ -266,46 +277,47 @@
                 for q in range(NY):
                     glin[t, h, b, :, q * QUART:q * QUART + ITEM] = gbuf[0, b, h, :, q * ITEM:(q + 1) * ITEM]
                     glin[t, h, b, :, q * QUART + ITEM:(q + 1) * QUART] = gbuf[1, q, h, :, b * ITEM:(b + 1) * ITEM]
-        g_core = send(glin.at[t, 1 - k], grecv.at[t], other)
+        g_core = copy(glin.at[t, 1 - k], grecv.at[t], other, mass_from, mass_sem)
+        g_core.start()
         midway()
-        g_core.wait_recv()
+        g_core.wait()
         for c in range(NX):
             gsum[t, c] = glin[t, k, c] + grecv[t, c]
-        g_x = [send(gsum.at[t, (x + d) % NX], g1recv.at[t, d - 1], xpeer(d)) for d in range(1, NX)]
-
-        second = []
+        for d in range(1, NX):
+            copy(gsum.at[t, (x + d) % NX], g1recv.at[t, d - 1], xpeer(d), mass_from, mass_sem + 1).start()
+
         for ty in range(2):
-            for d in range(1, 4):
-                plane_copy(ty, d).wait()
+            wait_arrived(lines(3 * SHARE), plane_sem + ty)
             part = sums[ty, me[ty], k]
             for n in range(3):
                 part = part + arecv[t, ty, n].astype(F32)
             a2f[ty] = part.reshape(4, ITEM, D)
             a2[t, ty] = part.astype(BF16).reshape(4, ITEM, D)
-            second.append([
-                send(a2.at[t, ty, (me[1 - ty] + d) % 4], a2recv.at[t, ty, d - 1], peer[1 - ty](d)) for d in (2, 1, 3)])
-        for c in g_x:
-            c.wait_recv()
+            for d in (2, 1, 3):
+                copy(a2.at[t, ty, (me[1 - ty] + d) % 4], a2recv.at[t, ty, d - 1], peer[1 - ty](d),
+                     second_from, second_sem + ty).start()
+        wait_arrived(g1recv.at[t], mass_sem + 1)
+        wait_sent(g1recv.at[t], mass_from)
         g = gsum[t, x]
         for n in range(NX - 1):
             g = g + g1recv[t, n]
         g2[t] = g
-        g_y = [send(g2.at[t], g2recv.at[t, d - 1], ypeer(d)) for d in range(1, NY)]
+        for d in range(1, NY):
+            copy(g2.at[t], g2recv.at[t, d - 1], ypeer(d), mass_from, mass_sem + 2).start()
         quarter = []
         for ty in range(2):
-            for c in second[ty]:
-                c.wait_recv()
+            wait_arrived(lines(3 * ITEM), second_sem + ty)
             whole = a2f[ty, me[1 - ty]]
             for n in range(3):
                 whole = whole + a2recv[t, ty, n].astype(F32)
             quarter.append(whole)
-        for c in g_y:
-            c.wait_recv()
+        wait_arrived(g2recv.at[t], mass_sem + 2)
+        wait_sent(g2recv.at[t], mass_from)
         for n in range(NY - 1):
             g = g + g2recv[t, n]
-        for j in range(4):
-            for ty in range(2):
-                core_copy(ty, j).wait_send()
+        wait_sent(sums.at[0], core_from)
+        wait_sent(lines(6 * SHARE), plane_from)
+        wait_sent(lines(6 * ITEM), second_from)
         return jnp.concatenate(quarter, axis=0), g
 
     place = pl.ds(pl.multiple_of(k * PART + y * QUART, QUART), QUART)
@@ -320,8 +332,8 @@
         m = column(mass)
         return (m * old + total) / (m + column(g))
 
-    hop, finish = ring(0)
-    hop2, finish2 = ring(1)
+    hop, finish = ring(0, 4)
+    hop2, finish2 = ring(1, 2)
     begin, go_on, arrive, on, finish_spread = spread(0)
     hop(1)
     begin((1,))
@@ -361,7 +373,7 @@
     early(2)
     finish()
     early(3)
-    finish_spread()
+    finish_spread((1,))
     normalise(0)
     hop2(1)
     total, g = reduce_sums(0, lambda: hop2(2))
@@ -400,26 +412,34 @@
         return 0
 
     lax.fori_loop(0, 5, late, 0)
-    finish_spread()
+    finish_spread((0, 1))
     normalise(1)
     total, g = reduce_sums(1, lambda: None)
     mass = massbuf[0, k]
     out[place, :] = update(cur[...], mass, total, g).astype(BF16)
-    around = [send(out.at[place], out.at[place], ypeer(d)) for d in (2, 1, 3)]
-    passed = [send(out.at[place], out.at[place], other)]
+    from_final, from_passed, from_mass = sender(), sender(), sender()
+    final_sem, passed_sem, new_sem = take(3), take(1), take(1)
+
+    def pass_on(d):
+        src = out.at[pl.ds(pl.multiple_of(k * PART + ((y + NY - d) % NY) * QUART, QUART), QUART)]
+        copy(src, src, other, from_passed, passed_sem).start()
+
+    for d in (2, 1, 3):
+        copy(out.at[place], out.at[place], ypeer(d), from_final, final_sem + d - 1).start()
+    pass_on(0)
     massbuf[1, k] = mass + g
-    passed.append(send(massbuf.at[1, k], massbuf.at[1, k], other))
-    for n, d in ((1, 1), (2, 3), (0, 2)):
-        around[n].wait_recv()
-        src = out.at[pl.ds(pl.multiple_of(k * PART + ((y + NY - d) % NY) * QUART, QUART), QUART)]
-        passed.append(send(src, src, other))
-    for c in passed:
-        c.wait_recv()
+    copy(massbuf.at[1, k], massbuf.at[1, k], other, from_mass, new_sem).start()
+    for d in (1, 3, 2):
+        wait_arrived(out.at[place], final_sem + d - 1)
+        pass_on(d)
+    wait_arrived(out.at[pl.ds(0, 4 * QUART)], passed_sem)
+    wait_arrived(massbuf.at[1, k], new_sem)
     for h in range(2):
         new_counts[h * PART:(h + 1) * PART] = massbuf[1, h][0]
-    for c in sent:
-        c.wait_send()
-    assert used[0] <= SEMS, used[0]
+    wait_sent(out.at[pl.ds(0, 3 * QUART)], from_final)
+    wait_sent(out.at[pl.ds(0, 4 * QUART)], from_passed)
+    wait_sent(massbuf.at[1, 0], from_mass)
+    assert used[0] <= SENDS and used[1] <= RECVS, used
 
 
 def body(batch, centroids, counts):
@@ -456,8 +476,8 @@
             pltpu.VMEM((2, NY - 1, 8, PART), F32),
             pltpu.VMEM((QUART, D), F32),
             pltpu.VMEM((2, 2, 8, PART), F32),
-            pltpu.SemaphoreType.DMA((SEMS,)),
-            pltpu.SemaphoreType.DMA((SEMS,)),
+            pltpu.SemaphoreType.DMA((SENDS,)),
+            pltpu.SemaphoreType.DMA((RECVS,)),
         ],
         compiler_params=pltpu.CompilerParams(
             collective_id=0, has_side_effects=True, vmem_limit_bytes=44 * 1024 * 1024

time: 116 us -> 113 us (0.974)
  Pallas kernels: 110 us -> 108 us
    pallas_call x1, Pallas kernels: 110 us -> 108 us  [body(): pl.pallas_call(kernel, out_shape=(jax.ShapeDtypeStruct((BLOCK, D), BF16),...]
where the time goes in v4:
time: 113 us
  Pallas kernels  108 us (96%)
  local copies, waits for them, and re-layouts  3.66 us (3%)
  other arithmetic  1.25 us (1%)
    pallas_call x1, Pallas kernels, body(): pl.pallas_call(kernel, out_shape=(jax.ShapeDtypeStruct((BLOCK, D), BF16),...  108 us
    unnamed x7, local copies, waits for them, and re-layouts  3.66 us

profile of v4, /device:TPU:1, one launch (start us, length us, event | category | flops | bytes accessed | tf_op | source)
XLA Modules:
  0.0 113.1 jit_solution(7180646566167802340)
XLA Ops:
  0.6 0.0 copy-start
  0.6 1.4 %copy-done = f32[512,768]{1,0:T(8,128)S(1)} copy-done((f32[512,768]{1,0:T(8,128)S(1)}, f32[512,768]{1,0:T(8,128)}, u32[]{:S(2)}) %copy-start) | copy-done | bytes 1572888
  2.0 0.0 copy-start.1
  2.0 1.0 copy-done.1
  3.0 0.0 copy-start.2
  3.0 0.7 copy-done.2
  3.7 107.5 %shard_map.50 = (bf16[512,768]{1,0:T(8,128)(2,1)S(1)}, f32[512]{0:T(512)S(1)}) custom-call(bf16[2,128,768]{2,1,0:T(8,128)(2,1)S(1)} %copy-done.1, f32[512,768]{1,0:T(8,128)S(1)} %copy-done, f32[512]{0:T(512)S(1)} %copy-done.2), custom_call_target="tpu_custom_call" | custom-call | tf_op jit(solution)/shard_map/pallas_call | solution.py:447
  111.2 1.3 %convert_element_type.3 = f32[512,768]{1,0:T(8,128)} convert(bf16[512,768]{1,0:T(8,128)(2,1)S(1)} %get-tuple-element.4) | non-fusion elementwise | flops 393216 | bytes 2359296 | tf_op jit(solution)/shard_map/convert_element_type | solution.py:486
  112.5 0.6 copy.6
Async XLA Ops:
  0.6 1.4 %copy-start = (f32[512,768]{1,0:T(8,128)S(1)}, f32[512,768]{1,0:T(8,128)}, u32[]{:S(2)}) copy-start(f32[512,768]{1,0:T(8,128)} %cents.1) | copy-start | bytes 4718596
  2.0 1.0 copy-start.1
  3.0 0.7 copy-start.2

commit v5 on v4

--- a/solution.py
+++ b/solution.py
@@ -23,8 +23,9 @@
 OWNERS = (-1, 1, -2, 2, -3, 3, 0, 4)
 
 
-def kernel(batch, cents, counts, out, new_counts, rows, cbuf, pbuf, mst, lst, stats, joint, sums, crecv, abuf, arecv,
-           a2, a2f, a2recv, gbuf, glin, grecv, gsum, g1recv, g2, g2recv, cur, massbuf, send_sem, recv_sem):
+def kernel(batch, cents_hbm, counts_hbm, out, new_counts, rows, cbuf, pbuf, mst, lst, stats, joint, sums, crecv, abuf, arecv,
+           a2, a2f, a2recv, gbuf, glin, grecv, gsum, g1recv, g2, g2recv, cur, massbuf, cents, counts, load_sem,
+           send_sem, recv_sem):
     dp = lax.axis_index("dp")
     ce = lax.axis_index("cent")
     y, k = dp // 2, dp % 2
@@ -73,27 +74,39 @@
     def items(i):
         return pl.ds(pl.multiple_of(i * ITEM, ITEM), ITEM)
 
+    def slot(h, sign):
+        return {0: 6, 4: 7}.get(h, 2 * h - 2 + (sign < 0)) * OWN
+
+    core_half = pl.ds(pl.multiple_of(k * PART, PART), PART)
+    own_rows = pl.ds(slot(0, 1), OWN)
+    loads = [
+        pltpu.make_async_copy(cents_hbm.at[core_half], cents, load_sem.at[0]),
+        pltpu.make_async_copy(batch.at[0], rows.at[0, own_rows], load_sem.at[1]),
+        pltpu.make_async_copy(batch.at[1], rows.at[1, own_rows], load_sem.at[2]),
+        pltpu.make_async_copy(counts_hbm, counts, load_sem.at[3]),
+    ]
+    for c in loads:
+        c.start()
+
     barrier = pltpu.get_barrier_semaphore()
     peers = [other]
     peers += [xpeer(d) for d in range(1, NX)]
     peers += [ypeer(d) for d in range(1, NY)]
-    peers += [zpeer(d) for d in range(1, NZ)]
+    peers += [zpeer(d) for d in (1, NZ - 1)]
     for p in peers:
         pl.semaphore_signal(barrier, inc=1, device_id=p, device_id_type=MESH)
 
-    def slot(h, sign):
-        return {0: 6, 4: 7}.get(h, 2 * h - 2 + (sign < 0)) * OWN
-
-    for t in range(2):
-        rows[t, slot(0, 1):slot(0, 1) + OWN, :] = batch[t]
+    loads[0].wait()
 
     def from_block(first):
-        return (cents[pl.ds(pl.multiple_of(k * PART + first, ITEM), ITEM), :] * SHARP).astype(BF16)
+        return (cents[pl.ds(pl.multiple_of(first, ITEM), ITEM), :] * SHARP).astype(BF16)
 
     for q in range(NY):
         cbuf[0, 0, x, k, q * ITEM:(q + 1) * ITEM, :] = from_block(q * QUART)
     cbuf[0, 1, y, k, items(x), :] = from_block(y * QUART + ITEM)
 
+    for c in loads[1:]:
+        c.wait()
     pl.semaphore_wait(barrier, len(peers))
 
     ring_from, ring_sem = sender(), take(28)
@@ -150,12 +163,12 @@
                 for d in (2, 1, 3):
                     far(ty, 0, d).start()
 
-        def go_on(types):
-            for ty in types:
+        def go_on(types, come):
+            for ty in come:
                 wait_arrived(lines(3 * ITEM), near_sem + ty)
             for d in (1, 3, 2):
                 for n in (1, 3, 2):
-                    for ty in range(2):
+                    for ty in types:
                         far(ty, n, d).start()
 
         def arrive(d, own):
@@ -279,7 +292,6 @@
                     glin[t, h, b, :, q * QUART + ITEM:(q + 1) * QUART] = gbuf[1, q, h, :, b * ITEM:(b + 1) * ITEM]
         g_core = copy(glin.at[t, 1 - k], grecv.at[t], other, mass_from, mass_sem)
         g_core.start()
-        midway()
         g_core.wait()
         for c in range(NX):
             gsum[t, c] = glin[t, k, c] + grecv[t, c]
@@ -296,6 +308,7 @@
             for d in (2, 1, 3):
                 copy(a2.at[t, ty, (me[1 - ty] + d) % 4], a2recv.at[t, ty, d - 1], peer[1 - ty](d),
                      second_from, second_sem + ty).start()
+        midway()
         wait_arrived(g1recv.at[t], mass_sem + 1)
         wait_sent(g1recv.at[t], mass_from)
         g = gsum[t, x]
@@ -321,6 +334,7 @@
         return jnp.concatenate(quarter, axis=0), g
 
     place = pl.ds(pl.multiple_of(k * PART + y * QUART, QUART), QUART)
+    quarter = pl.ds(pl.multiple_of(y * QUART, QUART), QUART)
     lane = lax.broadcasted_iota(jnp.int32, (QUART, PART), 1)
     line = lax.broadcasted_iota(jnp.int32, (QUART, PART), 0) + y * QUART
     hit = lane == line
@@ -332,14 +346,14 @@
         m = column(mass)
         return (m * old + total) / (m + column(g))
 
-    hop, finish = ring(0, 4)
+    hop, finish = ring(0, 2)
     hop2, finish2 = ring(1, 2)
     begin, go_on, arrive, on, finish_spread = spread(0)
     hop(1)
     begin((1,))
-    go_on((1,))
+    go_on((0, 1), (1,))
+    hop(2)
     arrive(0, True)
-    hop(2)
     arrive(1, False)
     arrive(3, False)
     hop(3)
@@ -378,7 +392,7 @@
     hop2(1)
     total, g = reduce_sums(0, lambda: hop2(2))
     mass = jnp.broadcast_to(counts[pl.ds(pl.multiple_of(k * PART, PART), PART)].reshape(1, PART), (8, PART))
-    fresh = update(cents[place, :], mass, total, g)
+    fresh = update(cents[quarter, :], mass, total, g)
     cur[...] = fresh
     massbuf[0, k] = mass + g
     fresh = (fresh * SHARP).astype(BF16)
@@ -387,7 +401,7 @@
     begin, go_on, arrive, on, finish_spread = spread(1)
     begin((0, 1))
     hop2(3)
-    go_on((0, 1))
+    go_on((0, 1), (0, 1))
     hop2(4)
     finish2()
 
@@ -450,7 +464,7 @@
             jax.ShapeDtypeStruct((BLOCK, D), BF16),
             jax.ShapeDtypeStruct((BLOCK,), F32),
         ),
-        in_specs=[vmem] * 3,
+        in_specs=[pl.BlockSpec(memory_space=pltpu.HBM)] * 3,
         out_specs=(vmem, vmem),
         scratch_shapes=[
             pltpu.VMEM((2, ROWS, D), BF16),
@@ -476,11 +490,14 @@
             pltpu.VMEM((2, NY - 1, 8, PART), F32),
             pltpu.VMEM((QUART, D), F32),
             pltpu.VMEM((2, 2, 8, PART), F32),
+            pltpu.VMEM((PART, D), F32),
+            pltpu.VMEM((BLOCK,), F32),
+            pltpu.SemaphoreType.DMA((4,)),
             pltpu.SemaphoreType.DMA((SENDS,)),
             pltpu.SemaphoreType.DMA((RECVS,)),
         ],
         compiler_params=pltpu.CompilerParams(
-            collective_id=0, has_side_effects=True, vmem_limit_bytes=44 * 1024 * 1024
+            collective_id=0, has_side_effects=True, vmem_limit_bytes=58 * 1024 * 1024
         ),
     )(batch, centroids, counts)
     return refined.astype(F32), mass

time: 113 us -> 111 us (0.982)
  local copies, waits for them, and re-layouts: 3.66 us -> 0.58 us
  other arithmetic: 1.25 us -> 2.39 us
    unnamed x7 -> x3, local copies, waits for them, and re-layouts: 3.66 us -> 0.58 us
    convert_element_type x1, other arithmetic: 1.25 us -> 2.39 us  [body(): return (refined.astype(F32), mass)]
where the time goes in v5:
time: 111 us
  Pallas kernels  108 us (97%)
  other arithmetic  2.39 us (2%)
    pallas_call x1, Pallas kernels, body(): pl.pallas_call(kernel, out_shape=(jax.ShapeDtypeStruct((BLOCK, D), BF16),...  108 us
    convert_element_type x1, other arithmetic, body(): return (refined.astype(F32), mass)  2.39 us

profile of v5, /device:TPU:1, one launch (start us, length us, event | category | flops | bytes accessed | tf_op | source)
XLA Modules:
  0.0 111.3 jit_solution(5114048242936104415)
XLA Ops:
  0.6 107.7 %shard_map.50 = (bf16[512,768]{1,0:T(8,128)(2,1)}, f32[512]{0:T(512)}) custom-call(bf16[2,128,768]{2,1,0:T(8,128)(2,1)} %batch.1, f32[512,768]{1,0:T(8,128)} %cents_hbm.1, f32[512]{0:T(512)} %counts_hbm.1), custom_call_target="tpu_custom_call" | custom-call | tf_op jit(solution)/shard_map/pallas_call | solution.py:461
  108.3 0.0 copy-start
  108.4 2.4 %convert_element_type.3 = f32[512,768]{1,0:T(8,128)} convert(bf16[512,768]{1,0:T(8,128)(2,1)} %get-tuple-element.4) | non-fusion elementwise | flops 393216 | bytes 2359296 | tf_op jit(solution)/shard_map/convert_element_type | solution.py:503
  110.7 0.0 copy-done
  110.7 0.6 copy.6
Async XLA Ops:
  108.3 2.4 %copy-start = (f32[512]{0:T(512)S(1)}, f32[512]{0:T(512)}, u32[]{:S(2)}) copy-start(f32[512]{0:T(512)} %get-tuple-element.9) | copy-start | bytes 6148

commit v6 on v5

--- a/solution.py
+++ b/solution.py
@@ -23,7 +23,7 @@
 OWNERS = (-1, 1, -2, 2, -3, 3, 0, 4)
 
 
-def kernel(batch, cents_hbm, counts_hbm, out, new_counts, rows, cbuf, pbuf, mst, lst, stats, joint, sums, crecv, abuf, arecv,
+def kernel(batch, cents_hbm, counts_hbm, out, new_counts, rows, cbuf, pbuf, mst, lst, stats, joint, sums, crecv, abuf, arecv, onward,
            a2, a2f, a2recv, gbuf, glin, grecv, gsum, g1recv, g2, g2recv, cur, massbuf, cents, counts, load_sem,
            send_sem, recv_sem):
     dp = lax.axis_index("dp")
@@ -223,7 +223,7 @@
         mst[...] = jnp.exp(m - joint[2:3, :]) / joint[3:4, :]
 
     core_from, plane_from, second_from, mass_from = sender(), sender(), sender(), sender()
-    core_sem, plane_sem, second_sem, mass_sem = take(8), take(2), take(2), take(3)
+    core_sem, onward_sem, plane_sem, second_sem, mass_sem = take(8), take(2), take(2), take(2), take(3)
 
     def reduce_sums(t, midway):
 
@@ -231,10 +231,20 @@
             i = target(ty, j)
             return copy(sums.at[ty, i, 1 - k], crecv.at[t, ty, i], other, core_from, core_sem + ty * 4 + j)
 
-        def plane_copy(ty, d):
-            i = (x + ty * (y - x) + d) % 4
+        def part_of(half):
+            return pl.ds(pl.multiple_of(half * (SHARE // 2), SHARE // 2), SHARE // 2)
+
+        def plane_copy(ty, d, target_of, half, dst, sem):
+            c = x + ty * (y - x)
+            i = (c + d) % 4
             to = at(x + (1 - ty) * (i - x), y + ty * (i - y), z, k)
-            return copy(abuf.at[t, ty, i], arecv.at[t, ty, d - 1], to, plane_from, plane_sem + ty)
+            return copy(abuf.at[t, ty, (c + target_of) % 4, part_of(half)], dst, to, plane_from, sem + ty)
+
+        def onward_copy(ty, half):
+            return plane_copy(ty, 1 + 2 * half, 2, half, onward.at[t, ty, half], onward_sem)
+
+        def last_copy(ty, d, half):
+            return plane_copy(ty, d, d, half, arecv.at[t, ty, d // 2, part_of(half)], plane_sem)
 
         def far_first(j):
             return (2 + j * (j + 1) // 2) % 4
@@ -250,9 +260,14 @@
             sums[ty, i, k] = whole
             abuf[t, ty, i] = whole.astype(BF16)
 
-            @pl.when(j < 3)
+            @pl.when(j == 0)
             def _():
-                plane_copy(ty, far_first(j)).start()
+                onward_copy(ty, 0).start()
+                onward_copy(ty, 1).start()
+
+            @pl.when((j == 1) | (j == 2))
+            def _():
+                last_copy(ty, far_first(j), j - 1).start()
 
         def body(n, _):
             ty, j = n % 2, n // 2
@@ -273,6 +288,13 @@
         lax.fori_loop(0, 8, body, 0)
         combine(6)
         combine(7)
+        for ty in range(2):
+            wait_arrived(lines(SHARE), onward_sem + ty)
+            for half, d in ((0, 1), (1, 3)):
+                i = (me[ty] + d) % 4
+                piece = slice(half * (SHARE // 2), (half + 1) * (SHARE // 2))
+                abuf[t, ty, i, piece, :] = (sums[ty, i, k, piece, :] + onward[t, ty, half].astype(F32)).astype(BF16)
+                last_copy(ty, d, half).start()
 
         def masses(n, _):
             ty, i = n // 4, n % 4
@@ -299,9 +321,9 @@
             copy(gsum.at[t, (x + d) % NX], g1recv.at[t, d - 1], xpeer(d), mass_from, mass_sem + 1).start()
 
         for ty in range(2):
-            wait_arrived(lines(3 * SHARE), plane_sem + ty)
+            wait_arrived(lines(2 * SHARE), plane_sem + ty)
             part = sums[ty, me[ty], k]
-            for n in range(3):
+            for n in range(2):
                 part = part + arecv[t, ty, n].astype(F32)
             a2f[ty] = part.reshape(4, ITEM, D)
             a2[t, ty] = part.astype(BF16).reshape(4, ITEM, D)
@@ -477,7 +499,8 @@
             pltpu.VMEM((2, 4, 2, SHARE, D), F32),
             pltpu.VMEM((2, 2, 4, SHARE, D), F32),
             pltpu.VMEM((2, 2, 4, SHARE, D), BF16),
-            pltpu.VMEM((2, 2, 3, SHARE, D), BF16),
+            pltpu.VMEM((2, 2, 2, SHARE, D), BF16),
+            pltpu.VMEM((2, 2, 2, SHARE // 2, D), BF16),
             pltpu.VMEM((2, 2, 4, ITEM, D), BF16),
             pltpu.VMEM((2, 4, ITEM, D), F32),
             pltpu.VMEM((2, 2, 3, ITEM, D), BF16),

time: 111 us -> 108 us (0.973)
  Pallas kernels: 108 us -> 104 us
    pallas_call x1, Pallas kernels: 108 us -> 104 us  [body(): pl.pallas_call(kernel, out_shape=(jax.ShapeDtypeStruct((BLOCK, D), BF16),...]
where the time goes in v6:
time: 108 us
  Pallas kernels  104 us (96%)
  other arithmetic  2.39 us (2%)
    pallas_call x1, Pallas kernels, body(): pl.pallas_call(kernel, out_shape=(jax.ShapeDtypeStruct((BLOCK, D), BF16),...  104 us
    convert_element_type x1, other arithmetic, body(): return (refined.astype(F32), mass)  2.39 us

profile of v6, /device:TPU:1, one launch (start us, length us, event | category | flops | bytes accessed | tf_op | source)
XLA Modules:
  0.0 107.5 jit_solution(8327891245321870365)
XLA Ops:
  0.6 103.9 %shard_map.50 = (bf16[512,768]{1,0:T(8,128)(2,1)}, f32[512]{0:T(512)}) custom-call(bf16[2,128,768]{2,1,0:T(8,128)(2,1)} %batch.1, f32[512,768]{1,0:T(8,128)} %cents_hbm.1, f32[512]{0:T(512)} %counts_hbm.1), custom_call_target="tpu_custom_call" | custom-call | tf_op jit(solution)/shard_map/pallas_call | solution.py:483
  104.6 0.0 copy-start
  104.6 2.4 %convert_element_type.3 = f32[512,768]{1,0:T(8,128)} convert(bf16[512,768]{1,0:T(8,128)(2,1)} %get-tuple-element.4) | non-fusion elementwise | flops 393216 | bytes 2359296 | tf_op jit(solution)/shard_map/convert_element_type | solution.py:526
  107.0 0.0 copy-done
  107.0 0.6 copy.6
Async XLA Ops:
  104.6 2.4 %copy-start = (f32[512]{0:T(512)S(1)}, f32[512]{0:T(512)}, u32[]{:S(2)}) copy-start(f32[512]{0:T(512)} %get-tuple-element.9) | copy-start | bytes 6148

commit v7 on v6

--- a/solution.py
+++ b/solution.py
@@ -109,7 +109,7 @@
         c.wait()
     pl.semaphore_wait(barrier, len(peers))
 
-    ring_from, ring_sem = sender(), take(28)
+    ring_from, ring_sem = sender(), take(14)
 
     def ring(t, parts):
         size = OWN // parts
@@ -140,7 +140,7 @@
         return hop, finish
 
     near_from, far_from, over_from = sender(), sender(), sender()
-    near_sem, far_sem, over_sem = take(2), take(6), take(8)
+    near_sem, far_sem, two_sem, over_sem = take(2), take(16), take(2), take(8)
 
     def spread(t):
         def near(ty, n):
@@ -149,7 +149,13 @@
 
         def far(ty, n, d):
             src = cbuf.at[t, ty, me[ty], k, items((me[1 - ty] + 4 - n) % 4)]
-            return copy(src, src, peer[ty](d), far_from, far_sem + ty * 3 + d - 1)
+            return copy(src, src, peer[ty](d), far_from, far_sem + ty * 8 + d // 2 * 4 + n)
+
+        def further(ty, n, d):
+            first = (me[1 - ty] + 4 - n) % 4 * ITEM + d // 2 * (ITEM // 2)
+            where = pl.ds(pl.multiple_of(first, ITEM // 2), ITEM // 2)
+            src = cbuf.at[t, ty, (me[ty] + 4 - d) % 4, k, where]
+            return copy(src, src, peer[ty](d), far_from, two_sem + ty)
 
         def on(ty, d):
             src = cbuf.at[t, ty, (me[ty] + 4 - d) % 4, k]
@@ -160,21 +166,27 @@
                 for n in (2, 1, 3):
                     near(ty, n).start()
             for ty in range(2):
-                for d in (2, 1, 3):
+                for d in (1, 3):
                     far(ty, 0, d).start()
 
         def go_on(types, come):
             for ty in come:
                 wait_arrived(lines(3 * ITEM), near_sem + ty)
-            for d in (1, 3, 2):
-                for n in (1, 3, 2):
+            for n in (1, 3, 2):
+                for d in (1, 3):
                     for ty in types:
                         far(ty, n, d).start()
 
-        def arrive(d, own):
+        def relay(n):
             for ty in range(2):
-                if not own:
-                    wait_arrived(lines(SHARE), far_sem + ty * 3 + d - 1)
+                for d in (1, 3):
+                    wait_arrived(lines(ITEM), far_sem + ty * 8 + d // 2 * 4 + n)
+                    further(ty, n, d).start()
+
+        def arrive(d):
+            for ty in range(2):
+                if d == 2:
+                    wait_arrived(lines(SHARE), two_sem + ty)
                 on(ty, d).start()
 
         def finish(types):
@@ -182,7 +194,7 @@
             wait_sent(lines(6 * SHARE), far_from)
             wait_sent(lines(8 * SHARE), over_from)
 
-        return begin, go_on, arrive, on, finish
+        return begin, go_on, relay, arrive, on, finish
 
     def score(t, ty, i, first, size):
         s = lax.dot_general(
@@ -370,16 +382,19 @@
 
     hop, finish = ring(0, 2)
     hop2, finish2 = ring(1, 2)
-    begin, go_on, arrive, on, finish_spread = spread(0)
+    begin, go_on, relay, arrive, on, finish_spread = spread(0)
     hop(1)
     begin((1,))
     go_on((0, 1), (1,))
     hop(2)
-    arrive(0, True)
-    arrive(1, False)
-    arrive(3, False)
+    relay(0)
+    arrive(0)
+    for n in (1, 3, 2):
+        relay(n)
+    arrive(1)
+    arrive(3)
     hop(3)
-    arrive(2, False)
+    arrive(2)
     hop(4)
 
     def early(b):
@@ -420,34 +435,32 @@
     fresh = (fresh * SHARP).astype(BF16)
     cbuf[1, 0, x, k, items(y), :] = fresh[:ITEM]
     cbuf[1, 1, y, k, items(x), :] = fresh[ITEM:]
-    begin, go_on, arrive, on, finish_spread = spread(1)
+    begin, go_on, relay, arrive, on, finish_spread = spread(1)
     begin((0, 1))
     hop2(3)
     go_on((0, 1), (0, 1))
+    arrive(0)
+    relay(0)
     hop2(4)
+    for n in (1, 3, 2):
+        relay(n)
+    arrive(1)
+    arrive(3)
     finish2()
 
     def late(j, _):
         d = near_first(j)
 
-        @pl.when(j == 0)
+        @pl.when(j == 3)
         def _():
-            arrive(d, True)
-
-        @pl.when((j > 0) & (j < 4))
-        def _():
-            arrive(d, False)
-
-        @pl.when(j > 0)
-        def _():
-            before = near_first(j - 1)
-            for ty in range(2):
-                on(ty, before).wait_recv()
-                score(1, ty, (me[ty] + 4 - before) % 4, 0, ROWS)
-
+            arrive(2)
+
+        for ty in range(2):
+            on(ty, d).wait_recv()
+            score(1, ty, (me[ty] + 4 - d) % 4, 0, ROWS)
         return 0
 
-    lax.fori_loop(0, 5, late, 0)
+    lax.fori_loop(0, 4, late, 0)
     finish_spread((0, 1))
     normalise(1)
     total, g = reduce_sums(1, lambda: None)

time: 108 us -> 105 us (0.972)
  Pallas kernels: 104 us -> 101 us
    pallas_call x1, Pallas kernels: 104 us -> 101 us  [body(): pl.pallas_call(kernel, out_shape=(jax.ShapeDtypeStruct((BLOCK, D), BF16),...]
where the time goes in v7:
time: 105 us
  Pallas kernels  101 us (96%)
  other arithmetic  2.39 us (2%)
    pallas_call x1, Pallas kernels, body(): pl.pallas_call(kernel, out_shape=(jax.ShapeDtypeStruct((BLOCK, D), BF16),...  101 us
    convert_element_type x1, other arithmetic, body(): return (refined.astype(F32), mass)  2.39 us

profile of v7, /device:TPU:1, one launch (start us, length us, event | category | flops | bytes accessed | tf_op | source)
XLA Modules:
  0.0 105.0 jit_solution(5010220503478709492)
XLA Ops:
  0.6 101.4 %shard_map.50 = (bf16[512,768]{1,0:T(8,128)(2,1)}, f32[512]{0:T(512)}) custom-call(bf16[2,128,768]{2,1,0:T(8,128)(2,1)} %batch.1, f32[512,768]{1,0:T(8,128)} %cents_hbm.1, f32[512]{0:T(512)} %counts_hbm.1), custom_call_target="tpu_custom_call" | custom-call | tf_op jit(solution)/shard_map/pallas_call | solution.py:496
  102.0 0.0 copy-start
  102.0 2.4 %convert_element_type.3 = f32[512,768]{1,0:T(8,128)} convert(bf16[512,768]{1,0:T(8,128)(2,1)} %get-tuple-element.4) | non-fusion elementwise | flops 393216 | bytes 2359296 | tf_op jit(solution)/shard_map/convert_element_type | solution.py:539
  104.4 0.0 copy-done
  104.4 0.6 copy.6
Async XLA Ops:
  102.0 2.4 %copy-start = (f32[512]{0:T(512)S(1)}, f32[512]{0:T(512)}, u32[]{:S(2)}) copy-start(f32[512]{0:T(512)} %get-tuple-element.9) | copy-start | bytes 6148

commit v8 on v7

--- a/solution.py
+++ b/solution.py
@@ -163,7 +163,7 @@
 
         def begin(types):
             for ty in types:
-                for n in (2, 1, 3):
+                for n in (1, 3, 2):
                     near(ty, n).start()
             for ty in range(2):
                 for d in (1, 3):

time: 105 us -> 106 us (level)
  no operation moved by 1% of the time
where the time goes in v8:
time: 106 us; the launch traced here: 105 us
  Pallas kernels  102 us (96%)
  other arithmetic  2.39 us (2%)
    pallas_call x1, Pallas kernels, body(): pl.pallas_call(kernel, out_shape=(jax.ShapeDtypeStruct((BLOCK, D), BF16),...  102 us
    convert_element_type x1, other arithmetic, body(): return (refined.astype(F32), mass)  2.39 us

profile of v8, /device:TPU:1, one launch (start us, length us, event | category | flops | bytes accessed | tf_op | source)
XLA Modules:
  0.0 105.5 jit_solution(5505700998808989065)
XLA Ops:
  0.6 101.9 %shard_map.50 = (bf16[512,768]{1,0:T(8,128)(2,1)}, f32[512]{0:T(512)}) custom-call(bf16[2,128,768]{2,1,0:T(8,128)(2,1)} %batch.1, f32[512,768]{1,0:T(8,128)} %cents_hbm.1, f32[512]{0:T(512)} %counts_hbm.1), custom_call_target="tpu_custom_call" | custom-call | tf_op jit(solution)/shard_map/pallas_call | solution.py:496
  102.5 0.0 copy-start
  102.5 2.4 %convert_element_type.3 = f32[512,768]{1,0:T(8,128)} convert(bf16[512,768]{1,0:T(8,128)(2,1)} %get-tuple-element.4) | non-fusion elementwise | flops 393216 | bytes 2359296 | tf_op jit(solution)/shard_map/convert_element_type | solution.py:539
  104.9 0.0 copy-done
  104.9 0.6 copy.6
Async XLA Ops:
  102.5 2.4 %copy-start = (f32[512]{0:T(512)S(1)}, f32[512]{0:T(512)}, u32[]{:S(2)}) copy-start(f32[512]{0:T(512)} %get-tuple-element.9) | copy-start | bytes 6148
